TPU v7x, 768 devices: a whole 4x8x12 slice. The times are simulated.
768 devices in a mesh: lon: 96 (over z_lo, y, core), lat: 8 (over z_hi, x).
Axes of the slice: x: 4, y: 8, z: 12 (z_hi: 2, z_lo: 6; z = z_hi * 6 + z_lo), core: 2. Of those that a mesh axis runs over, the one named last changes fastest.
Arguments:
- state: float32 [16, 512, 12288], P(None, 'lat', 'lon'), may hold values from -6 to 6
- land_mask: int32 [512, 12288], P('lat', 'lon'), may hold values from 0 to 1, as said below
- kernel_one: bfloat16 [3, 3, 16, 16], replicated, may hold values from -0.5 to 0.5
- bias_one: float32 [16], replicated, may hold values from -3 to 3
- kernel_two: bfloat16 [3, 3, 16, 16], replicated, may hold values from -0.5 to 0.5
- bias_two: float32 [16], replicated, may hold values from -3 to 3
- kernel_three: bfloat16 [3, 3, 8, 16], replicated, may hold values from -0.5 to 0.5
- bias_three: float32 [8], replicated, may hold values from -3 to 3
Outputs:
- updated: float32 [16, 512, 12288], P(None, 'lat', 'lon')
Inputs may be any that keep to these rules, and one draw needn't show every extreme that they name: `land_mask`: 1 marks an ocean cell and 0 land; whole tiles of 64 x 128 cells may be land.
All inputs are finite; a program needn't handle non-finite values.
Results may differ from a plain program's by a relative error of at most 0.0003.
Values sent between devices are 32-bit elements; how exact they have to be, the bound alone decides.
A program may use at most 128 MiB of HBM per device.

v0:
```python
import jax
import jax.numpy as jnp
from jax import lax
from jax.sharding import PartitionSpec as P


def padded_2(x, sides, width, wrap):
    for axis, dim in sides:
        size, length = (lax.axis_size(axis), x.shape[dim])
        up = [(i, (i + 1) % size) for i in range(size if wrap else size - 1)]
        down = [(j, i) for i, j in up]
        last = lax.slice_in_dim(x, length - width, length, axis=dim)
        leading = lax.slice_in_dim(x, 0, width, axis=dim)
        before = lax.ppermute(last, axis, up)
        after = lax.ppermute(leading, axis, down)
        x = jnp.concatenate([before, x, after], axis=dim)
    return x


def conv(x, kernel, bias):
    rows = x.shape[1] - 2
    cols = x.shape[2] - 2
    total = jnp.zeros((kernel.shape[2], rows, cols), jnp.float32) + bias[:, None, None]
    for a in range(3):
        for c in range(3):
            total = total + jnp.einsum(
                "ok,khw->ohw",
                kernel[a, c],
                x[:, a : a + rows, c : c + cols],
                preferred_element_type=jnp.float32,
            )
    return total


def fold_rows(state, wide):
    channels = state.shape[0]
    height = state.shape[1]
    flipped = wide[:, height - 3 :, :][:, ::-1, ::-1]
    count = lax.axis_size("lon")
    flat = flipped.reshape(count, flipped.size // count)
    mixed = lax.all_to_all(flat, "lon", split_axis=0, concat_axis=0, tiled=True)
    back = lax.all_to_all(mixed[::-1], "lon", split_axis=0, concat_axis=0, tiled=True)
    rows = back.reshape(flipped.shape)
    sign = jnp.where(jnp.arange(channels) < channels // 2, -1.0, 1.0).astype(jnp.float32)
    return rows * sign[:, None, None]


def step_tile(
    padded, state, ocean, kernel_one, bias_one, kernel_two, bias_two, kernel_three, bias_three
):
    channels = state.shape[0]
    levels = channels // 4
    layer_in = padded.astype(jnp.bfloat16)
    hidden_one = jax.nn.silu(conv(layer_in, kernel_one, bias_one)).astype(jnp.bfloat16)
    hidden_two = jax.nn.silu(conv(hidden_one, kernel_two, bias_two)).astype(jnp.bfloat16)
    forcing = conv(hidden_two, kernel_three, bias_three)
    centre = padded[:, 3:-3, 3:-3]
    east = padded[:, 3:-3, 4:-2]
    west = padded[:, 3:-3, 2:-4]
    north = padded[:, 4:-2, 3:-3]
    south_cells = padded[:, 2:-4, 3:-3]
    speed_u = jnp.tile(centre[0:levels], (4, 1, 1))
    speed_v = jnp.tile(centre[levels : 2 * levels], (4, 1, 1))
    tendency = -0.5 * (speed_u * (east - west) + speed_v * (north - south_cells))
    tendency = tendency + 0.2 * (east + west + north + south_cells - 4.0 * centre)
    extra = jnp.concatenate(
        [forcing, jnp.zeros((channels - forcing.shape[0],) + forcing.shape[1:], jnp.float32)],
        axis=0,
    )
    tendency = tendency + extra
    return state + 0.1 * ocean[None, :, :] * tendency


def shards(state, land_mask, kernel_one, bias_one, kernel_two, bias_two, kernel_three, bias_three):
    height = state.shape[1]
    at_top = lax.axis_index("lat") == lax.axis_size("lat") - 1
    widened = padded_2(state, (("lon", 2),), 3, True)
    tall = padded_2(widened, (("lat", 1),), 3, False)
    rows = fold_rows(state, widened)
    padded = jnp.concatenate(
        [tall[:, : height + 3], jnp.where(at_top, rows, tall[:, height + 3 :])], axis=1
    )
    ocean = land_mask.astype(jnp.float32)
    return step_tile(
        padded, state, ocean, kernel_one, bias_one, kernel_two, bias_two, kernel_three, bias_three
    )


def solution(mesh):
    return jax.shard_map(
        shards,
        mesh=mesh,
        in_specs=(P(None, "lat", "lon"), P("lat", "lon"), P(), P(), P(), P(), P(), P()),
        out_specs=P(None, "lat", "lon"),
        check_vma=False,
    )
```

profile of v0, /device:TPU:6, one launch (start us, length us, event | category | flops | bytes accessed | tf_op | source)
XLA Modules:
  0.0 134.8 jit_solution(12110870632271483470)
XLA Ops:
  0.0 1.3 %copy.137 = f32[16,64,128]{2,0,1:T(8,128)S(1)} copy(f32[16,64,128]{2,1,0:T(8,128)} %param.8) | data formatting | bytes 1048576 | tf_op args[0]
  1.6 15.1 %collective-permute-start = (f32[16,64,3]{2,0,1:T(8,128)S(1)}, f32[16,64,3]{2,0,1:T(8,128)S(1)}, u32[]{:S(2)}, u32[]{:S(2)}) collective-permute-start(f32[16,64,3]{2,0,1:T(8,128)S(1)} %get-tuple-element.32), channel_id=1, source_target_pairs={{8,0},{16,8},{24,16},{32,24},{40,32},{48,40},{56,48},{64,56},{72,6... | collective-permute-start | bytes 36872 | tf_op jit(solution)/shard_map/ppermute | solution.py:15
  16.6 1.9 %collective-permute-start.1 = (f32[16,64,3]{2,0,1:T(8,128)S(1)}, f32[16,64,3]{2,0,1:T(8,128)S(1)}, u32[]{:S(2)}, u32[]{:S(2)}) collective-permute-start(f32[16,64,3]{2,0,1:T(8,128)S(1)} %get-tuple-element.31), channel_id=1, source_target_pairs={{0,8},{8,16},{16,24},{24,32},{32,40},{40,48},{48,56},{56,64},{64,7... | collective-permute-start | bytes 36872 | tf_op jit(solution)/shard_map/ppermute | solution.py:14
  18.6 4.7 %collective-permute-done = f32[16,64,3]{2,0,1:T(8,128)S(1)} collective-permute-done((f32[16,64,3]{2,0,1:T(8,128)S(1)}, f32[16,64,3]{2,0,1:T(8,128)S(1)}, u32[]{:S(2)}, u32[]{:S(2)}) %collective-permute-start) | collective-permute-done | bytes 12320 | tf_op jit(solution)/shard_map/ppermute | solution.py:15
  23.3 10.7 %collective-permute-done.1 = f32[16,64,3]{2,0,1:T(8,128)S(1)} collective-permute-done((f32[16,64,3]{2,0,1:T(8,128)S(1)}, f32[16,64,3]{2,0,1:T(8,128)S(1)}, u32[]{:S(2)}, u32[]{:S(2)}) %collective-permute-start.1) | collective-permute-done | bytes 12320 | tf_op jit(solution)/shard_map/ppermute | solution.py:14
  35.2 0.7 all_to_all.14
  35.9 5.9 %all-to-all-start = ((f32[96,1,67]{2,1,0:T(1,128)}), f32[96,1,67]{2,1,0:T(1,128)S(1)}, u32[]{:S(2)}, u32[]{:S(2)}) async-start(f32[96,1,67]{2,1,0:T(1,128)} %bitcast.2), calls=%async_computation | async-start | bytes 98304 | tf_op jit(solution)/shard_map/all_to_all | solution.py:41
  41.8 0.6 convert_multiply_fusion
  42.4 9.9 %collective-permute-start.3 = (f32[16,3,134]{2,0,1:T(8,128)S(1)}, f32[16,3,134]{2,0,1:T(8,128)S(1)}, u32[]{:S(2)}, u32[]{:S(2)}) collective-permute-start(f32[16,3,134]{2,0,1:T(8,128)S(1)} %get-tuple-element.9), channel_id=1, source_target_pairs={{0,1},{1,2},{2,3},{3,4},{4,5},{5,6},{6,7},{8,9},{9,10},{10,11},{11... | collective-permute-start | bytes 77192 | tf_op jit(solution)/shard_map/ppermute | solution.py:14
  52.4 1.9 %collective-permute-start.2 = (f32[16,3,134]{2,0,1:T(8,128)S(1)}, f32[16,3,134]{2,0,1:T(8,128)S(1)}, u32[]{:S(2)}, u32[]{:S(2)}) collective-permute-start(f32[16,3,134]{2,0,1:T(8,128)S(1)} %get-tuple-element.10), channel_id=1, source_target_pairs={{1,0},{2,1},{3,2},{4,3},{5,4},{6,5},{7,6},{9,8},{10,9},{11,10},{12... | collective-permute-start | bytes 77192 | tf_op jit(solution)/shard_map/ppermute | solution.py:15
  54.5 0.6 rev.7
  55.1 13.7 %all-to-all-start.1 = ((f32[96,1,67]{2,1,0:T(1,128)}), f32[96,1,67]{2,1,0:T(1,128)S(1)}, u32[]{:S(2)}, u32[]{:S(2)}) async-start(f32[96,1,67]{2,1,0:T(1,128)} %bitcast.5), calls=%async_computation.1 | async-start | bytes 98304 | tf_op jit(solution)/shard_map/all_to_all | solution.py:42
  69.0 0.7 copy.112
  69.7 11.7 %all-to-all-done.1 = f32[96,1,67]{2,1,0:T(1,128)S(1)} async-done(((f32[96,1,67]{2,1,0:T(1,128)}), f32[96,1,67]{2,1,0:T(1,128)S(1)}, u32[]{:S(2)}, u32[]{:S(2)}) %all-to-all-start.1) | async-done | bytes 25760 | tf_op jit(solution)/shard_map/all_to_all | solution.py:42
  81.9 0.8 reduce.3
  82.8 0.7 fusion.68
  83.6 2.4 %fusion.71 = (bf16[16,68,132]{2,0,1:T(8,128)(2,1)S(1)}, bf16[16,68,132]{2,0,1:T(8,128)(2,1)S(1)}, bf16[16,68,132]{2,0,1:T(8,128)(2,1)S(1)}, bf16[16,68,132]{2,0,...) fusion(bf16[16,70,134]{2,0,1:T(8,128)(2,1)S(1)} %pad_maximum_fu, ...), kind=kLoop, calls=%fused_computation.113 | loop fusion | bytes 5170176 | tf_op jit(solution)/shard_map/slice | solution.py:29
  86.0 2.8 %copy.119 = bf16[16,68,132]{1,0,2:T(8,128)(2,1)} copy(bf16[16,68,132]{2,0,1:T(8,128)(2,1)} %get-tuple-element.19) | data formatting | bytes 574464 | tf_op jit(solution)/shard_map/slice | solution.py:29
  88.8 2.8 %copy.120 = bf16[16,68,132]{1,0,2:T(8,128)(2,1)} copy(bf16[16,68,132]{2,0,1:T(8,128)(2,1)} %get-tuple-element.18) | data formatting | bytes 574464 | tf_op jit(solution)/shard_map/slice | solution.py:29
  91.6 2.8 %copy.121 = bf16[16,68,132]{1,0,2:T(8,128)(2,1)} copy(bf16[16,68,132]{2,0,1:T(8,128)(2,1)} %get-tuple-element.17) | data formatting | bytes 574464 | tf_op jit(solution)/shard_map/slice | solution.py:29
  94.4 2.8 %copy.122 = bf16[16,68,132]{1,0,2:T(8,128)(2,1)} copy(bf16[16,68,132]{2,0,1:T(8,128)(2,1)} %get-tuple-element.16) | data formatting | bytes 574464 | tf_op jit(solution)/shard_map/slice | solution.py:29
  97.3 1.7 %copy.123 = bf16[16,68,132]{1,0,2:T(8,128)(2,1)} copy(bf16[16,68,132]{2,0,1:T(8,128)(2,1)S(1)} %get-tuple-element.15) | data formatting | bytes 574464 | tf_op jit(solution)/shard_map/slice | solution.py:29
  99.0 1.7 %copy.124 = bf16[16,68,132]{1,0,2:T(8,128)(2,1)} copy(bf16[16,68,132]{2,0,1:T(8,128)(2,1)S(1)} %get-tuple-element.14) | data formatting | bytes 574464 | tf_op jit(solution)/shard_map/slice | solution.py:29
  100.8 1.0 copy.125
  101.8 1.0 copy.126
  102.7 1.0 copy.127
  104.1 0.7 copy-done.5
  105.1 0.8 copy-done.4
  106.1 0.8 copy-done.3
  107.2 0.8 copy-done.2
  108.2 0.8 copy-done.1
  109.9 0.7 multiply_convert_fusion
  113.3 0.5 multiply_convert_fusion.1
  113.9 2.2 %fusion.72 = (bf16[16,64,128]{1,0,2:T(8,128)(2,1)S(1)}, bf16[16,64,128]{1,0,2:T(8,128)(2,1)S(1)}, bf16[16,64,128]{1,0,2:T(8,128)(2,1)S(1)}, bf16[16,64,128]{1,0,...) fusion(bf16[16,66,130]{1,0,2:T(8,128)(2,1)S(1)} %multiply_conve, ...), kind=kLoop, calls=%fused_computation.114 | loop fusion | bytes 4718592 | tf_op jit(solution)/shard_map/slice | solution.py:29
  116.0 2.3 %copy.128 = bf16[16,64,128]{2,0,1:T(8,128)(2,1)} copy(bf16[16,64,128]{1,0,2:T(8,128)(2,1)} %get-tuple-element.28) | data formatting | bytes 524288 | tf_op jit(solution)/shard_map/slice | solution.py:29
  118.3 2.3 %copy.129 = bf16[16,64,128]{2,0,1:T(8,128)(2,1)} copy(bf16[16,64,128]{1,0,2:T(8,128)(2,1)} %get-tuple-element.27) | data formatting | bytes 524288 | tf_op jit(solution)/shard_map/slice | solution.py:29
  120.6 2.3 %copy.130 = bf16[16,64,128]{2,0,1:T(8,128)(2,1)} copy(bf16[16,64,128]{1,0,2:T(8,128)(2,1)} %get-tuple-element.26) | data formatting | bytes 524288 | tf_op jit(solution)/shard_map/slice | solution.py:29
  122.9 2.3 %copy.131 = bf16[16,64,128]{2,0,1:T(8,128)(2,1)} copy(bf16[16,64,128]{1,0,2:T(8,128)(2,1)} %get-tuple-element.25) | data formatting | bytes 524288 | tf_op jit(solution)/shard_map/slice | solution.py:29
  125.2 0.6 copy.132
  125.8 0.6 copy.133
  126.4 0.6 copy.134
  127.0 0.6 copy.135
  127.6 0.6 copy.136
  128.3 0.9 convolution_add_fusion.26
  129.2 0.8 convolution_add_fusion.25
  130.0 0.8 convolution_add_fusion.24
  133.0 0.9 multiply_add_fusion
  133.9 1.0 copy.138
  (89 shorter events, 9.3 us)
Async XLA Ops:
  1.4 17.2 %copy-start.10 = (f32[16,64,128]{2,1,0:T(8,128)S(1)}, f32[16,64,128]{2,1,0:T(8,128)}, u32[]{:S(2)}) copy-start(f32[16,64,128]{2,1,0:T(8,128)} %param.8) | copy-start | bytes 1572868
  1.6 21.8 %collective-permute-start = (f32[16,64,3]{2,0,1:T(8,128)S(1)}, f32[16,64,3]{2,0,1:T(8,128)S(1)}, u32[]{:S(2)}, u32[]{:S(2)}) collective-permute-start(f32[16,64,3]{2,0,1:T(8,128)S(1)} %get-tuple-element.32), channel_id=1, source_target_pairs={{8,0},{16,8},{24,16},{32,24},{40,32},{48,40},{56,48},{64,56},{72,6... | collective-permute-start | bytes 36872 | tf_op jit(solution)/shard_map/ppermute | solution.py:15
  16.6 17.4 %collective-permute-start.1 = (f32[16,64,3]{2,0,1:T(8,128)S(1)}, f32[16,64,3]{2,0,1:T(8,128)S(1)}, u32[]{:S(2)}, u32[]{:S(2)}) collective-permute-start(f32[16,64,3]{2,0,1:T(8,128)S(1)} %get-tuple-element.31), channel_id=1, source_target_pairs={{0,8},{8,16},{16,24},{24,32},{32,40},{40,48},{48,56},{56,64},{64,7... | collective-permute-start | bytes 36872 | tf_op jit(solution)/shard_map/ppermute | solution.py:14
  18.6 23.2 %copy-start.20 = (s32[64,128]{1,0:T(8,128)S(1)}, s32[64,128]{1,0:T(8,128)}, u32[]{:S(2)}) copy-start(s32[64,128]{1,0:T(8,128)} %param.9) | copy-start | bytes 98308
  23.3 11.2 %copy-start.6 = (f32[16,64,3]{2,0,1:T(8,128)}, f32[16,64,3]{2,0,1:T(8,128)S(1)}, u32[]{:S(2)}) copy-start(f32[16,64,3]{2,0,1:T(8,128)S(1)} %collective-permute-done) | copy-start | bytes 36868
  34.1 0.8 copy-start.8
  35.9 18.6 %all-to-all-start = ((f32[96,1,67]{2,1,0:T(1,128)}), f32[96,1,67]{2,1,0:T(1,128)S(1)}, u32[]{:S(2)}, u32[]{:S(2)}) async-start(f32[96,1,67]{2,1,0:T(1,128)} %bitcast.2), calls=%async_computation | async-start | bytes 98304 | tf_op jit(solution)/shard_map/all_to_all | solution.py:41
  42.4 27.3 %collective-permute-start.3 = (f32[16,3,134]{2,0,1:T(8,128)S(1)}, f32[16,3,134]{2,0,1:T(8,128)S(1)}, u32[]{:S(2)}, u32[]{:S(2)}) collective-permute-start(f32[16,3,134]{2,0,1:T(8,128)S(1)} %get-tuple-element.9), channel_id=1, source_target_pairs={{0,1},{1,2},{2,3},{3,4},{4,5},{5,6},{6,7},{8,9},{9,10},{10,11},{11... | collective-permute-start | bytes 77192 | tf_op jit(solution)/shard_map/ppermute | solution.py:14
  52.4 30.4 %collective-permute-start.2 = (f32[16,3,134]{2,0,1:T(8,128)S(1)}, f32[16,3,134]{2,0,1:T(8,128)S(1)}, u32[]{:S(2)}, u32[]{:S(2)}) collective-permute-start(f32[16,3,134]{2,0,1:T(8,128)S(1)} %get-tuple-element.10), channel_id=1, source_target_pairs={{1,0},{2,1},{3,2},{4,3},{5,4},{6,5},{7,6},{9,8},{10,9},{11,10},{12... | collective-permute-start | bytes 77192 | tf_op jit(solution)/shard_map/ppermute | solution.py:15
  55.1 26.2 %all-to-all-start.1 = ((f32[96,1,67]{2,1,0:T(1,128)}), f32[96,1,67]{2,1,0:T(1,128)S(1)}, u32[]{:S(2)}, u32[]{:S(2)}) async-start(f32[96,1,67]{2,1,0:T(1,128)} %bitcast.5), calls=%async_computation.1 | async-start | bytes 98304 | tf_op jit(solution)/shard_map/all_to_all | solution.py:42
  69.7 13.8 %copy-start.16 = (f32[16,3,134]{2,0,1:T(8,128)}, f32[16,3,134]{2,0,1:T(8,128)S(1)}, u32[]{:S(2)}) copy-start(f32[16,3,134]{2,0,1:T(8,128)S(1)} %collective-permute-done.3) | copy-start | bytes 77188
  101.7 2.0 %copy-start = (bf16[16,68,132]{1,0,2:T(8,128)(2,1)S(1)}, bf16[16,68,132]{1,0,2:T(8,128)(2,1)}, u32[]{:S(2)}) copy-start(bf16[16,68,132]{1,0,2:T(8,128)(2,1)} %copy.119) | copy-start | bytes 861700
  101.7 2.0 %copy-start.21 = (bf16[3,3,16,16]{3,2,1,0:T(8,128)(2,1)S(1)}, bf16[3,3,16,16]{3,2,1,0:T(8,128)(2,1)}, u32[]{:S(2)}) copy-start(bf16[3,3,16,16]{3,2,1,0:T(8,128)(2,1)} %param.10) | copy-start | bytes 13828
  101.8 2.0 %copy-start.24 = (f32[16]{0:T(128)S(1)}, f32[16]{0:T(128)}, u32[]{:S(2)}) copy-start(f32[16]{0:T(128)} %param.11) | copy-start | bytes 196
  103.8 1.0 copy-start.5
  104.8 1.0 copy-start.4
  105.9 1.0 copy-start.3
  106.9 1.0 copy-start.2
  108.0 1.0 copy-start.1
  109.9 0.8 copy-start.22
  109.9 0.8 copy-start.25
  126.4 1.8 %copy-start.14 = (bf16[16,64,128]{2,0,1:T(8,128)(2,1)S(1)}, bf16[16,64,128]{2,0,1:T(8,128)(2,1)}, u32[]{:S(2)}) copy-start(bf16[16,64,128]{2,0,1:T(8,128)(2,1)} %copy.128) | copy-start | bytes 786436
  126.4 1.8 %copy-start.26 = (f32[8]{0:T(128)S(1)}, f32[8]{0:T(128)}, u32[]{:S(2)}) copy-start(f32[8]{0:T(128)} %param.15) | copy-start | bytes 100
  127.0 2.2 %copy-start.13 = (bf16[16,64,128]{2,0,1:T(8,128)(2,1)S(1)}, bf16[16,64,128]{2,0,1:T(8,128)(2,1)}, u32[]{:S(2)}) copy-start(bf16[16,64,128]{2,0,1:T(8,128)(2,1)} %copy.129) | copy-start | bytes 786436
  127.6 2.4 %copy-start.12 = (bf16[16,64,128]{2,0,1:T(8,128)(2,1)S(1)}, bf16[16,64,128]{2,0,1:T(8,128)(2,1)}, u32[]{:S(2)}) copy-start(bf16[16,64,128]{2,0,1:T(8,128)(2,1)} %copy.130) | copy-start | bytes 786436
  128.2 2.7 %copy-start.11 = (bf16[16,64,128]{2,0,1:T(8,128)(2,1)S(1)}, bf16[16,64,128]{2,0,1:T(8,128)(2,1)}, u32[]{:S(2)}) copy-start(bf16[16,64,128]{2,0,1:T(8,128)(2,1)} %copy.131) | copy-start | bytes 786436
  128.3 2.7 %copy-start.23 = (bf16[3,3,8,16]{3,2,1,0:T(8,128)(2,1)S(1)}, bf16[3,3,8,16]{3,2,1,0:T(8,128)(2,1)}, u32[]{:S(2)}) copy-start(bf16[3,3,8,16]{3,2,1,0:T(8,128)(2,1)} %param.14) | copy-start | bytes 6916
  131.6 0.9 copy-start.15
  131.8 1.1 copy-start.7
  131.8 1.2 copy-start.9
  131.8 1.2 copy-start.17
  131.8 1.2 copy-start.18
  131.8 1.2 copy-start.19
where the time goes:
time: 136 us; the launch traced here: 135 us
  starting transfers between devices  48.5 us (36%)
  local copies, waits for them, and re-layouts  45.2 us (33%)
  waiting for transfers between devices  27.3 us (20%)
  matrix products  9.58 us (7%)
  other arithmetic  3.54 us (3%)
    slice x20, local copies, waits for them, and re-layouts, conv(): x[:, a:a + rows, c:c + cols]  34.4 us
    ppermute x2, starting transfers between devices, padded_2(): after = lax.ppermute(leading, axis, down)  17 us
    all_to_all x1, starting transfers between devices, fold_rows(): lax.all_to_all(mixed[::-1], 'lon', split_axis=0, concat_axis=0, tiled=True)  13.7 us
    ppermute x2, starting transfers between devices, padded_2(): before = lax.ppermute(last, axis, up)  11.9 us
    all_to_all x1, waiting for transfers between devices, fold_rows(): lax.all_to_all(mixed[::-1], 'lon', split_axis=0, concat_axis=0, tiled=True)  11.7 us
    ppermute x2, waiting for transfers between devices, padded_2(): before = lax.ppermute(last, axis, up)  10.7 us
    dot_general x27, matrix products, conv(): jnp.einsum('ok,khw->ohw', kernel[a, c], x[:, a:a + rows, c:c + cols], pre...  9.58 us
    unnamed x57, local copies, waits for them, and re-layouts  6.72 us
  transfers between devices with their start and end apart: 6, of which 4 were waited for; matrix products, arithmetic and copies ran while one was open for 3% of the time, Pallas kernels for 0%

commit v1 on v0

v1 whole, which is shorter than its diff:
```python
import functools

import jax
import jax.numpy as jnp
from jax import lax
from jax.experimental import pallas as pl
from jax.experimental.pallas import tpu as pltpu
from jax.sharding import PartitionSpec as P

MESH = pl.DeviceIdType.MESH
F32, BF16 = jnp.float32, jnp.bfloat16
HW, HE, HS, HN, BS, BN, SW, SE, NW, NE = range(10)


def iota(shape, dim):
    return lax.broadcasted_iota(jnp.int32, shape, dim)


def silu(v):
    half = 0.5 * v
    return half + half * jnp.tanh(half)


def roll(x, shift, axis):
    return pltpu.roll(x, shift % x.shape[axis], axis)


def bands(taps, spread, band):
    outs = taps.shape[2]
    spreading = (iota((16, 128), 0) == iota((16, 128), 1) // 8).astype(BF16)
    flat = taps[...].reshape(9 * outs, 16)
    spread[0 : 9 * outs, :] = jnp.dot(flat, spreading, preferred_element_type=F32)
    ahead = iota((8, 128), 1) % 8 - iota((8, 128), 0)
    for c in range(3):
        for pair in range(8):
            parts = []
            for o in (2 * pair, 2 * pair + 1):
                if o >= outs:
                    parts.append(jnp.zeros((8, 384), F32))
                    continue
                tap = []
                for a in range(3):
                    at = (a * 3 + c) * outs + o
                    tap.append(jnp.broadcast_to(spread[at : at + 1, :], (8, 128)))
                before = jnp.where(ahead == 7, tap[0], 0.0)
                centre = jnp.where(
                    ahead == -1,
                    tap[0],
                    jnp.where(ahead == 0, tap[1], jnp.where(ahead == 1, tap[2], 0.0)),
                )
                after = jnp.where(ahead == -7, tap[2], 0.0)
                parts.append(jnp.concatenate([before, centre, after], axis=1))
            at = c * 128 + pair * 16
            band[at : at + 16, :] = jnp.concatenate(parts, axis=0).astype(BF16)


def across(y, outs):
    parts = []
    for at in range(0, y.shape[1], 128):
        z = y[:, at : at + 128]
        parts.append(
            roll(z[0:outs], 1, 1) + z[outs : 2 * outs] + roll(z[2 * outs : 3 * outs], -1, 1)
        )
    return parts


def down(y, groups):
    z = [y[:, 128 * c : 128 * c + 128].reshape(groups, 32, 128) for c in range(3)]
    return roll(z[0], 1, 1) + z[1] + roll(z[2], -1, 1)


def kernel(
    lon_count,
    lat_count,
    state,
    land_mask,
    kernel_one,
    bias_one,
    kernel_two,
    bias_two,
    kernel_three,
    bias_three,
    out,
    own,
    mask,
    taps_one,
    taps_two,
    taps_three,
    b_one,
    b_two,
    b_three,
    south,
    north,
    edges,
    west_cols,
    east_cols,
    south_edges,
    north_edges,
    corner_sw,
    corner_se,
    corner_nw,
    corner_ne,
    fold_rows,
    fold_edges,
    spread,
    band_one,
    band_two,
    band_three,
    bias_full,
    hidden_a,
    hidden_b,
    in_sems,
    send_sems,
    recv_sems,
):
    t, j = lax.axis_index("lon"), lax.axis_index("lat")
    top = lat_count - 1
    east, west = lax.rem(t + 1, lon_count), lax.rem(t + lon_count - 1, lon_count)
    mirror = lon_count - 1 - t
    mirror_up = lax.rem(mirror + 1, lon_count)
    mirror_down = lax.rem(mirror + lon_count - 1, lon_count)

    loads = [
        pltpu.make_async_copy(src, dst, in_sems.at[i])
        for i, (src, dst) in enumerate(
            [
                (state, own.at[:, 8:72, :]),
                (land_mask, mask),
                (kernel_one, taps_one),
                (kernel_two, taps_two),
                (kernel_three, taps_three),
                (bias_one, b_one),
                (bias_two, b_two),
                (bias_three, b_three),
            ]
        )
    ]
    for load in loads:
        load.start()

    south[...] = jnp.zeros_like(south)
    north[...] = jnp.zeros_like(north)
    south_edges[...] = jnp.zeros_like(south_edges)
    corner_sw[...] = jnp.zeros_like(corner_sw)
    corner_se[...] = jnp.zeros_like(corner_se)

    barrier = pltpu.get_barrier_semaphore()

    def greet(lon, lat):
        pl.semaphore_signal(barrier, inc=1, device_id={"lon": lon, "lat": lat}, device_id_type=MESH)

    greet(east, j)
    greet(west, j)

    @pl.when(j > 0)
    def _():
        greet(t, j - 1)
        greet(east, j - 1)
        greet(west, j - 1)

    @pl.when(j < top)
    def _():
        greet(t, j + 1)
        greet(east, j + 1)
        greet(west, j + 1)

    @pl.when(j == top)
    def _():
        greet(mirror, j)

        @pl.when(mirror_up != t)
        def _():
            greet(mirror_up, j)

        @pl.when(mirror_down != t)
        def _():
            greet(mirror_down, j)

    own[:, 0:8, :] = jnp.zeros((16, 8, 128), F32)
    own[:, 72:80, :] = jnp.zeros((16, 8, 128), F32)
    zeros = jnp.zeros((128, 128), BF16)
    for ref in (hidden_a, hidden_b):
        ref[0:128, :] = zeros
        ref[1152:1280, :] = zeros

    loads[0].wait()

    for g in range(8):
        turned = own[:, 8 * g + 8 : 8 * g + 16, :].reshape(128, 128).T
        edges[0:8, 128 * g : 128 * g + 128] = turned[120:128]
        edges[8:16, 128 * g : 128 * g + 128] = turned[0:8]

    @pl.when(j == top)
    def _():
        back = 127 - iota((8, 128), 1)
        up = 7 - iota((8, 128), 0)
        for ch in range(16):
            x = own[ch, 64:72, :]
            x = jnp.take_along_axis(x, back, axis=1)
            x = jnp.take_along_axis(x, up, axis=0)
            fold_rows[ch] = -x if ch < 8 else x
        lane = iota((8, 128), 1)
        rows_back = lane + 7 - 2 * (lane % 8)
        for at in (0, 8):
            x = edges[at : at + 8, 896:1024]
            x = jnp.take_along_axis(x, rows_back, axis=1)
            x = jnp.take_along_axis(x, up, axis=0)
            fold_edges[8 - at : 16 - at, :] = jnp.where(lane < 64, -x, x)

    partners = 2 + 3 * (j > 0).astype(jnp.int32)
    partners += jnp.where(
        j < top,
        3,
        1 + (mirror_up != t).astype(jnp.int32) + (mirror_down != t).astype(jnp.int32),
    )
    pl.semaphore_wait(barrier, partners)

    def copy(src, dst, slot, sender, lon, lat):
        return pltpu.make_async_remote_copy(
            src_ref=src,
            dst_ref=dst,
            send_sem=send_sems.at[sender],
            recv_sem=recv_sems.at[slot],
            device_id={"lon": lon, "lat": lat},
            device_id_type=MESH,
        )

    first, last = pl.ds(0, 128), pl.ds(896, 128)
    lon_copies = [
        copy(edges.at[0:8, :], west_cols, HW, 0, east, j),
        copy(edges.at[8:16, :], east_cols, HE, 1, west, j),
    ]
    south_copies = [
        copy(own.at[:, 8:11, :], north.at[:, 0:3, :], HN, 2, t, j - 1),
        copy(edges.at[:, first], north_edges, BN, 3, t, j - 1),
        copy(edges.at[0:8, first], corner_nw, NW, 4, east, j - 1),
        copy(edges.at[8:16, first], corner_ne, NE, 5, west, j - 1),
    ]
    north_copies = [
        copy(own.at[:, 69:72, :], south.at[:, 5:8, :], HS, 6, t, j + 1),
        copy(edges.at[:, last], south_edges, BS, 7, t, j + 1),
        copy(edges.at[0:8, last], corner_sw, SW, 8, east, j + 1),
        copy(edges.at[8:16, last], corner_se, SE, 9, west, j + 1),
    ]
    fold_copies = [
        copy(fold_rows.at[:, 0:3, :], north.at[:, 0:3, :], HN, 6, mirror, j),
        copy(fold_edges, north_edges, BN, 7, mirror, j),
    ]
    fold_up = copy(fold_edges.at[0:8, :], corner_nw, NW, 8, mirror_up, j)
    fold_down = copy(fold_edges.at[8:16, :], corner_ne, NE, 9, mirror_down, j)

    @pl.when(j == top)
    def _():
        for c in fold_copies:
            c.start()

        @pl.when(mirror_up != t)
        def _():
            fold_up.start()

        @pl.when(mirror_up == t)
        def _():
            corner_nw[...] = fold_edges[0:8, :]

        @pl.when(mirror_down != t)
        def _():
            fold_down.start()

        @pl.when(mirror_down == t)
        def _():
            corner_ne[...] = fold_edges[8:16, :]

    @pl.when(j < top)
    def _():
        for c in north_copies:
            c.start()

    @pl.when(j > 0)
    def _():
        for c in south_copies:
            c.start()

    for c in lon_copies:
        c.start()

    for load in loads[1:]:
        load.wait()
    bands(taps_one, spread, band_one)
    bands(taps_two, spread, band_two)
    bands(taps_three, spread, band_three)
    lane_out = iota((1, 128), 1) // 8
    bias_rows = []
    for i, (ref, outs) in enumerate(((b_one, 16), (b_two, 16), (b_three, 8))):
        row = jnp.zeros((1, 128), F32)
        for o in range(outs):
            bias_full[i, 8 * o : 8 * o + 8, :] = jnp.full((8, 128), ref[o], F32)
            row = jnp.where(lane_out == o, ref[o], row)
        bias_rows.append(row)

    for g in range(8):
        x = own[:, 8 * g + 8 : 8 * g + 16, :].reshape(128, 128)
        hidden_a[128 * g + 128 : 128 * g + 256, :] = x.astype(BF16)

    band_last = jnp.concatenate(
        [band_three[128 * c : 128 * c + 64, :] for c in range(3)], axis=0
    )

    def windows(ref, g):
        return jnp.concatenate(
            [ref[128 * g : 128 * g + 384, :], ref[128 * g + 128 : 128 * g + 512, :]], axis=1
        )

    for src, band, i, dst in (
        (hidden_a, band_one, 0, hidden_b),
        (hidden_b, band_two, 1, hidden_a),
    ):
        for g in range(0, 8, 2):
            y = jnp.dot(band[...], windows(src, g), preferred_element_type=F32)
            for h, v in enumerate(across(y, 128)):
                at = 128 * (g + h) + 128
                dst[at : at + 128, :] = silu(v + bias_full[i]).astype(BF16)

    lane = iota((8, 128), 1)
    row = iota((8, 128), 0)
    for g in range(0, 8, 2):
        y = jnp.dot(band_last, windows(hidden_a, g), preferred_element_type=F32)
        for h, v in enumerate(across(y, 64)):
            inner = (lane >= 3) & (lane < 125)
            if g + h == 0:
                inner = inner & (row >= 3)
            if g + h == 7:
                inner = inner & (row < 5)
            forcing = jnp.where(inner[None], (v + bias_full[2, 0:64, :]).reshape(8, 8, 128), 0.0)
            at = 8 * (g + h)
            x = own[:, at + 8 : at + 16, :]
            qn = own[:, at + 9 : at + 17, :]
            qs = own[:, at + 7 : at + 15, :]
            qe = jnp.where(lane[None] < 127, roll(x, -1, 2), 0.0)
            qw = jnp.where(lane[None] > 0, roll(x, 1, 2), 0.0)
            u = jnp.concatenate([x[0:4]] * 4, axis=0)
            w = jnp.concatenate([x[4:8]] * 4, axis=0)
            tendency = -0.5 * (u * (qe - qw) + w * (qn - qs))
            tendency = tendency + 0.2 * (qe + qw + qn + qs - 4.0 * x)
            tendency = jnp.concatenate([tendency[0:8] + forcing, tendency[8:16]], axis=0)
            ocean = 0.1 * mask[at : at + 8, :].astype(F32)
            out[:, at : at + 8, :] = x + ocean[None] * tendency

    @pl.when(j > 0)
    def _():
        for c in (north_copies[0], north_copies[1], north_copies[2], north_copies[3]):
            c.wait_recv()

    fold_copies[0].wait_recv()
    fold_copies[1].wait_recv()

    @pl.when((j < top) | (mirror_up != t))
    def _():
        fold_up.wait_recv()

    @pl.when((j < top) | (mirror_down != t))
    def _():
        fold_down.wait_recv()

    for c in lon_copies:
        c.wait_recv()

    strip = jnp.concatenate(
        [
            jnp.concatenate([south[...], own[:, 64:72, :]], axis=2).reshape(128, 256),
            jnp.concatenate([own[:, 8:16, :], north[...]], axis=2).reshape(128, 256),
        ],
        axis=0,
    ).astype(BF16)
    cols = [
        jnp.concatenate(
            [corner_sw[...], south_edges[8:16, :], south_edges[0:8, :], corner_se[...]], axis=0
        )
    ]
    for g in range(8):
        at = pl.ds(128 * g, 128)
        cols.append(
            jnp.concatenate(
                [west_cols[:, at], edges[8:16, at], edges[0:8, at], east_cols[:, at]], axis=0
            )
        )
    cols.append(
        jnp.concatenate(
            [corner_nw[...], north_edges[8:16, :], north_edges[0:8, :], corner_ne[...]], axis=0
        )
    )
    cols = [x.astype(BF16) for x in cols]

    def sides(cols, band, groups):
        none = jnp.zeros((32, 128), BF16)
        padded = [none] + cols + [none]
        lhs = jnp.concatenate(
            [jnp.concatenate(padded[g : g + 3], axis=1) for g in groups], axis=0
        )
        y = lax.dot_general(
            lhs, band[...], (((1,), (1,)), ((), ())), preferred_element_type=F32
        )
        return down(y, len(groups))

    for band, i in ((band_one, 0), (band_two, 1)):
        halves = []
        for at in (128, 0):
            y = jnp.dot(band[:, at : at + 256], strip, preferred_element_type=F32)
            bias = bias_full[i]
            halves.append(
                jnp.concatenate([silu(v + bias).astype(BF16) for v in across(y, 128)], axis=1)
            )
        strip = jnp.concatenate(halves, axis=0)
        y = silu(sides(cols, band, range(10)) + bias_rows[i][None]).astype(BF16)
        cols = [y[g] for g in range(10)]

    bias = bias_full[2, 0:64, :]
    y = jnp.dot(band_last[:, 0:256], strip[:, 0:128], preferred_element_type=F32)
    forcing_south = (across(y, 64)[0] + bias).reshape(8, 8, 128)
    y = jnp.dot(band_last[:, 128:384], strip[:, 128:256], preferred_element_type=F32)
    forcing_north = (across(y, 64)[0] + bias).reshape(8, 8, 128)
    forcing_sides = sides(cols, band_three, range(1, 9)) + bias_rows[2][None]

    place = iota((8, 128), 0)
    lane = iota((8, 128), 1)
    patches = []
    for g in range(8):
        at = pl.ds(128 * g, 128)

        def speed(x):
            x = jnp.where(lane < 32, x, 0.0)
            x = x + roll(x, 32, 1)
            return x + roll(x, 64, 1)

        e = edges[0:8, at]
        w = edges[8:16, at]
        east_term = jnp.where(place == 7, (0.2 - 0.5 * speed(e)) * roll(east_cols[:, at], -1, 0), 0.0)
        west_term = jnp.where(place == 0, (0.2 + 0.5 * speed(w)) * roll(west_cols[:, at], 1, 0), 0.0)
        patches.append(forcing_sides[g, 16:24] + east_term)
        patches.append(forcing_sides[g, 8:16] + west_term)
    turned = jnp.concatenate(patches, axis=0).T
    inner = (lane >= 3) & (lane < 125)
    for g in range(8):
        patch = roll(turned, 120 - 16 * g, 1).reshape(16, 8, 128)
        patch = jnp.where(inner[None], 0.0, patch)
        if g in (0, 7):
            x = own[:, 8 * g + 8 : 8 * g + 16, :]
            v = jnp.concatenate([x[4:8]] * 4, axis=0)
            if g == 0:
                near = jnp.where(place[None] == 0, (0.2 + 0.5 * v) * roll(south[...], 1, 1), 0.0)
                forcing = jnp.where((inner & (place < 3))[None], forcing_south, 0.0)
            else:
                near = jnp.where(place[None] == 7, (0.2 - 0.5 * v) * roll(north[...], -1, 1), 0.0)
                forcing = jnp.where((inner & (place >= 5))[None], forcing_north, 0.0)
            patch = patch + near
            patch = jnp.concatenate([patch[0:8] + forcing, patch[8:16]], axis=0)
        at = 8 * g
        ocean = 0.1 * mask[at : at + 8, :].astype(F32)
        out[:, at : at + 8, :] = out[:, at : at + 8, :] + ocean[None] * patch

    @pl.when(j == top)
    def _():
        for c in fold_copies:
            c.wait_send()

        @pl.when(mirror_up != t)
        def _():
            fold_up.wait_send()

        @pl.when(mirror_down != t)
        def _():
            fold_down.wait_send()

    @pl.when(j < top)
    def _():
        for c in north_copies:
            c.wait_send()

    @pl.when(j > 0)
    def _():
        for c in south_copies:
            c.wait_send()

    for c in lon_copies:
        c.wait_send()


def solution(mesh):
    lon_count, lat_count = mesh.shape["lon"], mesh.shape["lat"]

    def step(*args):
        state, *rest = [pltpu.with_memory_space_constraint(x, pltpu.HBM) for x in args]
        return pl.pallas_call(
            functools.partial(kernel, lon_count, lat_count),
            out_shape=jax.ShapeDtypeStruct(state.shape, F32),
            in_specs=[pl.BlockSpec(memory_space=pltpu.HBM)] * 8,
            out_specs=pl.BlockSpec(memory_space=pltpu.VMEM),
            scratch_shapes=[
                pltpu.VMEM((16, 80, 128), F32),
                pltpu.VMEM((64, 128), jnp.int32),
                pltpu.VMEM((3, 3, 16, 16), BF16),
                pltpu.VMEM((3, 3, 16, 16), BF16),
                pltpu.VMEM((3, 3, 8, 16), BF16),
                pltpu.SMEM((16,), F32),
                pltpu.SMEM((16,), F32),
                pltpu.SMEM((8,), F32),
                pltpu.VMEM((16, 8, 128), F32),
                pltpu.VMEM((16, 8, 128), F32),
                pltpu.VMEM((16, 1024), F32),
                pltpu.VMEM((8, 1024), F32),
                pltpu.VMEM((8, 1024), F32),
                pltpu.VMEM((16, 128), F32),
                pltpu.VMEM((16, 128), F32),
                pltpu.VMEM((8, 128), F32),
                pltpu.VMEM((8, 128), F32),
                pltpu.VMEM((8, 128), F32),
                pltpu.VMEM((8, 128), F32),
                pltpu.VMEM((16, 8, 128), F32),
                pltpu.VMEM((16, 128), F32),
                pltpu.VMEM((144, 128), F32),
                pltpu.VMEM((384, 384), BF16),
                pltpu.VMEM((384, 384), BF16),
                pltpu.VMEM((384, 384), BF16),
                pltpu.VMEM((3, 128, 128), F32),
                pltpu.VMEM((1280, 128), BF16),
                pltpu.VMEM((1280, 128), BF16),
                pltpu.SemaphoreType.DMA((8,)),
                pltpu.SemaphoreType.DMA((10,)),
                pltpu.SemaphoreType.DMA((10,)),
            ],
            compiler_params=pltpu.CompilerParams(
                collective_id=0, has_side_effects=True, vmem_limit_bytes=32 * 1024 * 1024
            ),
        )(state, *rest)

    return jax.shard_map(
        step,
        mesh=mesh,
        in_specs=(P(None, "lat", "lon"), P("lat", "lon"), P(), P(), P(), P(), P(), P()),
        out_specs=P(None, "lat", "lon"),
        check_vma=False,
    )
```

time: 136 us -> 27.7 us (0.20)
  starting transfers between devices: 48.5 us -> 0 us
  local copies, waits for them, and re-layouts: 45.2 us -> 0.8 us
  waiting for transfers between devices: 27.3 us -> 0 us
  Pallas kernels: 0 us -> 26.5 us
  matrix products: 9.58 us -> 0 us
  other arithmetic: 3.54 us -> 0 us
    slice x25 -> x0, local copies, waits for them, and re-layouts: 35.4 us -> none  [the longest x20 34.4 us: conv(): x[:, a:a + rows, c:c + cols]]
    ppermute x4 -> x0, starting transfers between devices: 28.8 us -> none  [the longest x2 17 us: padded_2(): after = lax.ppermute(leading, axis, down)]
    pallas_call x0 -> x1, Pallas kernels: none -> 26.5 us  [step(): pl.pallas_call(functools.partial(kernel, lon_count, lat_count), out_shape...]
    all_to_all x2 -> x0, starting transfers between devices: 19.6 us -> none  [the longest x1 13.7 us: fold_rows(): lax.all_to_all(mixed[::-1], 'lon', split_axis=0, concat_axis=0, tiled=True)]
    ppermute x4 -> x0, waiting for transfers between devices: 15.4 us -> none  [the longest x2 10.7 us: padded_2(): before = lax.ppermute(last, axis, up)]
    all_to_all x2 -> x0, waiting for transfers between devices: 11.9 us -> none  [the longest x1 11.7 us: fold_rows(): lax.all_to_all(mixed[::-1], 'lon', split_axis=0, concat_axis=0, tiled=True)]
    dot_general x27 -> x0, matrix products: 9.58 us -> none  [conv(): jnp.einsum('ok,khw->ohw', kernel[a, c], x[:, a:a + rows, c:c + cols], pre...]
    unnamed x57 -> x1, local copies, waits for them, and re-layouts: 6.72 us -> 0.8 us
  transfers between devices with their start and end apart: 6 -> 0, of which waited for: 4 -> 0; matrix products, arithmetic and copies ran while one was open for 3% -> 0% of each run, Pallas kernels for 0% -> 0%
where the time goes in v1:
time: 27.7 us; the launch traced here: 27.3 us
  Pallas kernels  26.5 us (96%)
  local copies, waits for them, and re-layouts  0.8 us (3%)
    pallas_call x1, Pallas kernels, step(): pl.pallas_call(functools.partial(kernel, lon_count, lat_count), out_shape...  26.5 us
    unnamed x1, local copies, waits for them, and re-layouts  0.8 us

profile of v1, /device:TPU:6, one launch (start us, length us, event | category | flops | bytes accessed | tf_op | source)
XLA Modules:
  0.0 27.3 jit_solution(1363928254581242597)
XLA Ops:
  0.0 26.5 %shard_map.82 = f32[16,64,128]{2,1,0:T(8,128)S(1)} custom-call(f32[16,64,128]{2,1,0:T(8,128)} %state.1, s32[64,128]{1,0:T(8,128)} %land_mask.1, bf16[3,3,16,16]{3,2,1,0:T(8,128)(2,1)} %kernel_one.1, f32[16]{0:T(128)} %bias_one.1, bf16[3,3,16,16]{3,2,1,0:T(8,128)(2,1)} %kernel_two.1, f32[16]{0:T(128)} %bias_two.1, bf16[3,3,8,16]{3,2,1,0:T(8,128)(2,1)} %kernel_three.1, ...), custom_call_target="tpu_custom_call" | custom-call | tf_op jit(solution)/shard_map/pallas_call | solution.py:492
  26.5 0.8 %copy.10 = f32[16,64,128]{2,1,0:T(8,128)} copy(f32[16,64,128]{2,1,0:T(8,128)S(1)} %shard_map.82) | data formatting | bytes 1048576

commit v2 on v1

--- a/solution.py
+++ b/solution.py
@@ -112,6 +112,7 @@
     in_sems,
     send_sems,
     recv_sems,
+    answers,
 ):
     t, j = lax.axis_index("lon"), lax.axis_index("lat")
     top = lat_count - 1
@@ -144,37 +145,94 @@
     corner_sw[...] = jnp.zeros_like(corner_sw)
     corner_se[...] = jnp.zeros_like(corner_se)
 
+    def rank(lon, lat):
+        z, y, x, core = (lat // 4) * 6 + lon // 16, (lon % 16) // 2, lat % 4, lon % 2
+        guess = jnp.where(z < 6, 14 * z, 60 + 5 * z) + 6 * jnp.minimum(y, 9 - y) + 4 * x + 4 * (1 - core)
+        guess = guess + jnp.where(lon + lat == 0, 100, 0)
+        return guess * 1024 + lat * lon_count + lon
+
+    mine = rank(t, j)
+    first, last = pl.ds(0, 128), pl.ds(896, 128)
+
+    def copy(src, dst, slot, sender, lon, lat):
+        return pltpu.make_async_remote_copy(
+            src_ref=src,
+            dst_ref=dst,
+            send_sem=send_sems.at[sender],
+            recv_sem=recv_sems.at[slot],
+            device_id={"lon": lon, "lat": lat},
+            device_id_type=MESH,
+        )
+
+    class Route:
+        def __init__(self, there, lon, lat, here, yonder, *copies):
+            self.there, self.lon, self.lat, self.here, self.yonder = there, lon, lat, here, yonder
+            theirs = rank(lon, lat)
+            self.greets = there & (mine < theirs)
+            self.answers = there & (mine > theirs)
+            self.far = theirs - mine > 25 * 1024
+            self.copies = [copy(*c, lon, lat) for c in copies]
+
+        def signal(self, sem):
+            pl.semaphore_signal(
+                sem, inc=1, device_id={"lon": self.lon, "lat": self.lat}, device_id_type=MESH
+            )
+
+        def send(self):
+            for c in self.copies:
+                c.start()
+
+    below, above, fold = j > 0, j < top, j == top
+    routes = [
+        Route(
+            below, t, j - 1, 2, 3,
+            (own.at[:, 8:11, :], north.at[:, 0:3, :], HN, 2),
+            (edges.at[:, first], north_edges, BN, 3),
+        ),
+        Route(below, east, j - 1, 4, 7, (edges.at[0:8, first], corner_nw, NW, 4)),
+        Route(below, west, j - 1, 5, 6, (edges.at[8:16, first], corner_ne, NE, 5)),
+        Route(
+            above, t, j + 1, 3, 2,
+            (own.at[:, 69:72, :], south.at[:, 5:8, :], HS, 6),
+            (edges.at[:, last], south_edges, BS, 7),
+        ),
+        Route(above, east, j + 1, 6, 5, (edges.at[0:8, last], corner_sw, SW, 8)),
+        Route(above, west, j + 1, 7, 4, (edges.at[8:16, last], corner_se, SE, 9)),
+        Route(
+            fold, mirror, j, 3, 3,
+            (fold_rows.at[:, 0:3, :], north.at[:, 0:3, :], HN, 6),
+            (fold_edges, north_edges, BN, 7),
+        ),
+        Route(
+            fold & (mirror_down != t), mirror_down, j, 6, 6,
+            (fold_edges.at[8:16, :], corner_ne, NE, 9),
+        ),
+        Route(
+            fold & (mirror_up != t), mirror_up, j, 7, 7,
+            (fold_edges.at[0:8, :], corner_nw, NW, 8),
+        ),
+        Route(j >= 0, east, j, 0, 1, (edges.at[5:8, :], west_cols.at[5:8, :], HW, 0)),
+        Route(j >= 0, west, j, 1, 0, (edges.at[8:11, :], east_cols.at[0:3, :], HE, 1)),
+    ]
+
     barrier = pltpu.get_barrier_semaphore()
-
-    def greet(lon, lat):
-        pl.semaphore_signal(barrier, inc=1, device_id={"lon": lon, "lat": lat}, device_id_type=MESH)
-
-    greet(east, j)
-    greet(west, j)
-
-    @pl.when(j > 0)
-    def _():
-        greet(t, j - 1)
-        greet(east, j - 1)
-        greet(west, j - 1)
-
-    @pl.when(j < top)
-    def _():
-        greet(t, j + 1)
-        greet(east, j + 1)
-        greet(west, j + 1)
-
-    @pl.when(j == top)
-    def _():
-        greet(mirror, j)
-
-        @pl.when(mirror_up != t)
+    greeted = jnp.int32(0)
+    for route in routes:
+        greeted = greeted + route.answers.astype(jnp.int32)
+
+        @pl.when(route.greets)
         def _():
-            greet(mirror_up, j)
-
-        @pl.when(mirror_down != t)
+            route.signal(barrier)
+
+    @pl.when(greeted > 0)
+    def _():
+        pl.semaphore_wait(barrier, greeted)
+
+    for route in routes:
+
+        @pl.when(route.answers)
         def _():
-            greet(mirror_down, j)
+            route.signal(answers.at[route.yonder])
 
     own[:, 0:8, :] = jnp.zeros((16, 8, 128), F32)
     own[:, 72:80, :] = jnp.zeros((16, 8, 128), F32)
@@ -190,7 +248,7 @@
         edges[0:8, 128 * g : 128 * g + 128] = turned[120:128]
         edges[8:16, 128 * g : 128 * g + 128] = turned[0:8]
 
-    @pl.when(j == top)
+    @pl.when(fold)
     def _():
         back = 127 - iota((8, 128), 1)
         up = 7 - iota((8, 128), 0)
@@ -207,81 +265,16 @@
             x = jnp.take_along_axis(x, up, axis=0)
             fold_edges[8 - at : 16 - at, :] = jnp.where(lane < 64, -x, x)
 
-    partners = 2 + 3 * (j > 0).astype(jnp.int32)
-    partners += jnp.where(
-        j < top,
-        3,
-        1 + (mirror_up != t).astype(jnp.int32) + (mirror_down != t).astype(jnp.int32),
-    )
-    pl.semaphore_wait(barrier, partners)
-
-    def copy(src, dst, slot, sender, lon, lat):
-        return pltpu.make_async_remote_copy(
-            src_ref=src,
-            dst_ref=dst,
-            send_sem=send_sems.at[sender],
-            recv_sem=recv_sems.at[slot],
-            device_id={"lon": lon, "lat": lat},
-            device_id_type=MESH,
-        )
-
-    first, last = pl.ds(0, 128), pl.ds(896, 128)
-    lon_copies = [
-        copy(edges.at[0:8, :], west_cols, HW, 0, east, j),
-        copy(edges.at[8:16, :], east_cols, HE, 1, west, j),
-    ]
-    south_copies = [
-        copy(own.at[:, 8:11, :], north.at[:, 0:3, :], HN, 2, t, j - 1),
-        copy(edges.at[:, first], north_edges, BN, 3, t, j - 1),
-        copy(edges.at[0:8, first], corner_nw, NW, 4, east, j - 1),
-        copy(edges.at[8:16, first], corner_ne, NE, 5, west, j - 1),
-    ]
-    north_copies = [
-        copy(own.at[:, 69:72, :], south.at[:, 5:8, :], HS, 6, t, j + 1),
-        copy(edges.at[:, last], south_edges, BS, 7, t, j + 1),
-        copy(edges.at[0:8, last], corner_sw, SW, 8, east, j + 1),
-        copy(edges.at[8:16, last], corner_se, SE, 9, west, j + 1),
-    ]
-    fold_copies = [
-        copy(fold_rows.at[:, 0:3, :], north.at[:, 0:3, :], HN, 6, mirror, j),
-        copy(fold_edges, north_edges, BN, 7, mirror, j),
-    ]
-    fold_up = copy(fold_edges.at[0:8, :], corner_nw, NW, 8, mirror_up, j)
-    fold_down = copy(fold_edges.at[8:16, :], corner_ne, NE, 9, mirror_down, j)
-
-    @pl.when(j == top)
-    def _():
-        for c in fold_copies:
-            c.start()
-
-        @pl.when(mirror_up != t)
-        def _():
-            fold_up.start()
-
-        @pl.when(mirror_up == t)
-        def _():
-            corner_nw[...] = fold_edges[0:8, :]
-
-        @pl.when(mirror_down != t)
-        def _():
-            fold_down.start()
-
-        @pl.when(mirror_down == t)
-        def _():
-            corner_ne[...] = fold_edges[8:16, :]
-
-    @pl.when(j < top)
-    def _():
-        for c in north_copies:
-            c.start()
-
-    @pl.when(j > 0)
-    def _():
-        for c in south_copies:
-            c.start()
-
-    for c in lon_copies:
-        c.start()
+    for route in routes:
+        pl.when(route.answers)(route.send)
+
+    @pl.when(fold & (mirror_up == t))
+    def _():
+        corner_nw[...] = fold_edges[0:8, :]
+
+    @pl.when(fold & (mirror_down == t))
+    def _():
+        corner_ne[...] = fold_edges[8:16, :]
 
     for load in loads[1:]:
         load.wait()
@@ -296,6 +289,13 @@
             bias_full[i, 8 * o : 8 * o + 8, :] = jnp.full((8, 128), ref[o], F32)
             row = jnp.where(lane_out == o, ref[o], row)
         bias_rows.append(row)
+
+    for route in routes:
+
+        @pl.when(route.greets & ~route.far)
+        def _():
+            pl.semaphore_wait(answers.at[route.here], 1)
+            route.send()
 
     for g in range(8):
         x = own[:, 8 * g + 8 : 8 * g + 16, :].reshape(128, 128)
@@ -345,24 +345,36 @@
             ocean = 0.1 * mask[at : at + 8, :].astype(F32)
             out[:, at : at + 8, :] = x + ocean[None] * tendency
 
-    @pl.when(j > 0)
-    def _():
-        for c in (north_copies[0], north_copies[1], north_copies[2], north_copies[3]):
-            c.wait_recv()
-
-    fold_copies[0].wait_recv()
-    fold_copies[1].wait_recv()
-
-    @pl.when((j < top) | (mirror_up != t))
-    def _():
-        fold_up.wait_recv()
-
-    @pl.when((j < top) | (mirror_down != t))
-    def _():
-        fold_down.wait_recv()
-
-    for c in lon_copies:
-        c.wait_recv()
+    for route in routes:
+
+        @pl.when(route.greets & route.far)
+        def _():
+            pl.semaphore_wait(answers.at[route.here], 1)
+            route.send()
+
+    def arrive(dst, slot):
+        copy(dst, dst, slot, 0, east, j).wait_recv()
+
+    arrive(west_cols.at[5:8, :], HW)
+    arrive(east_cols.at[0:3, :], HE)
+
+    @pl.when(below)
+    def _():
+        arrive(south.at[:, 5:8, :], HS)
+        arrive(south_edges, BS)
+        arrive(corner_sw, SW)
+        arrive(corner_se, SE)
+
+    arrive(north.at[:, 0:3, :], HN)
+    arrive(north_edges, BN)
+
+    @pl.when(above | (mirror_up != t))
+    def _():
+        arrive(corner_nw, NW)
+
+    @pl.when(above | (mirror_down != t))
+    def _():
+        arrive(corner_ne, NE)
 
     strip = jnp.concatenate(
         [
@@ -457,31 +469,12 @@
         ocean = 0.1 * mask[at : at + 8, :].astype(F32)
         out[:, at : at + 8, :] = out[:, at : at + 8, :] + ocean[None] * patch
 
-    @pl.when(j == top)
-    def _():
-        for c in fold_copies:
-            c.wait_send()
-
-        @pl.when(mirror_up != t)
+    for route in routes:
+
+        @pl.when(route.there)
         def _():
-            fold_up.wait_send()
-
-        @pl.when(mirror_down != t)
-        def _():
-            fold_down.wait_send()
-
-    @pl.when(j < top)
-    def _():
-        for c in north_copies:
-            c.wait_send()
-
-    @pl.when(j > 0)
-    def _():
-        for c in south_copies:
-            c.wait_send()
-
-    for c in lon_copies:
-        c.wait_send()
+            for c in route.copies:
+                c.wait_send()
 
 
 def solution(mesh):
@@ -526,6 +519,7 @@
                 pltpu.SemaphoreType.DMA((8,)),
                 pltpu.SemaphoreType.DMA((10,)),
                 pltpu.SemaphoreType.DMA((10,)),
+                pltpu.SemaphoreType.REGULAR((8,)),
             ],
             compiler_params=pltpu.CompilerParams(
                 collective_id=0, has_side_effects=True, vmem_limit_bytes=32 * 1024 * 1024

time: 27.7 us -> 23.6 us (0.85); the launches traced: 27.3 us -> 23.5 us
  Pallas kernels: 26.5 us -> 22.7 us
    pallas_call x1, Pallas kernels: 26.5 us -> 22.7 us  [step(): pl.pallas_call(functools.partial(kernel, lon_count, lat_count), out_shape...]
where the time goes in v2:
time: 23.6 us; the launch traced here: 23.5 us
  Pallas kernels  22.7 us (96%)
  local copies, waits for them, and re-layouts  0.8 us (3%)
    pallas_call x1, Pallas kernels, step(): pl.pallas_call(functools.partial(kernel, lon_count, lat_count), out_shape...  22.7 us
    unnamed x1, local copies, waits for them, and re-layouts  0.8 us

profile of v2, /device:TPU:6, one launch (start us, length us, event | category | flops | bytes accessed | tf_op | source)
XLA Modules:
  0.0 23.5 jit_solution(1345773362395427568)
XLA Ops:
  0.0 22.7 %shard_map.82 = f32[16,64,128]{2,1,0:T(8,128)S(1)} custom-call(f32[16,64,128]{2,1,0:T(8,128)} %state.1, s32[64,128]{1,0:T(8,128)} %land_mask.1, bf16[3,3,16,16]{3,2,1,0:T(8,128)(2,1)} %kernel_one.1, f32[16]{0:T(128)} %bias_one.1, bf16[3,3,16,16]{3,2,1,0:T(8,128)(2,1)} %kernel_two.1, f32[16]{0:T(128)} %bias_two.1, bf16[3,3,8,16]{3,2,1,0:T(8,128)(2,1)} %kernel_three.1, ...), custom_call_target="tpu_custom_call" | custom-call | tf_op jit(solution)/shard_map/pallas_call | solution.py:485
  22.7 0.8 %copy.10 = f32[16,64,128]{2,1,0:T(8,128)} copy(f32[16,64,128]{2,1,0:T(8,128)S(1)} %shard_map.82) | data formatting | bytes 1048576

commit v3 on v2

--- a/solution.py
+++ b/solution.py
@@ -9,7 +9,7 @@
 
 MESH = pl.DeviceIdType.MESH
 F32, BF16 = jnp.float32, jnp.bfloat16
-HW, HE, HS, HN, BS, BN, SW, SE, NW, NE = range(10)
+HW, HE, HS, HN, SW, SE, NW, NE = range(8)
 
 
 def iota(shape, dim):
@@ -94,8 +94,6 @@
     edges,
     west_cols,
     east_cols,
-    south_edges,
-    north_edges,
     corner_sw,
     corner_se,
     corner_nw,
@@ -125,7 +123,9 @@
         pltpu.make_async_copy(src, dst, in_sems.at[i])
         for i, (src, dst) in enumerate(
             [
-                (state, own.at[:, 8:72, :]),
+                (state.at[:, 0:8, :], own.at[:, 8:16, :]),
+                (state.at[:, 56:64, :], own.at[:, 64:72, :]),
+                (state.at[:, 8:56, :], own.at[:, 16:64, :]),
                 (land_mask, mask),
                 (kernel_one, taps_one),
                 (kernel_two, taps_two),
@@ -139,16 +139,11 @@
     for load in loads:
         load.start()
 
-    south[...] = jnp.zeros_like(south)
-    north[...] = jnp.zeros_like(north)
-    south_edges[...] = jnp.zeros_like(south_edges)
-    corner_sw[...] = jnp.zeros_like(corner_sw)
-    corner_se[...] = jnp.zeros_like(corner_se)
-
     def rank(lon, lat):
         z, y, x, core = (lat // 4) * 6 + lon // 16, (lon % 16) // 2, lat % 4, lon % 2
-        guess = jnp.where(z < 6, 14 * z, 60 + 5 * z) + 6 * jnp.minimum(y, 9 - y) + 4 * x + 4 * (1 - core)
-        guess = guess + jnp.where(lon + lat == 0, 100, 0)
+        guess = jnp.where(z < 6, 128 + 150 * z, 940 + 30 * z) + 45 * x - 41 * core
+        guess = guess + jnp.where(y < 4, 57 * y, 430 - 35 * y)
+        guess = jnp.where(lon + lat == 0, 1050, guess)
         return guess * 1024 + lat * lon_count + lon
 
     mine = rank(t, j)
@@ -165,12 +160,17 @@
         )
 
     class Route:
-        def __init__(self, there, lon, lat, here, yonder, *copies):
+        def __init__(self, there, lon, lat, here, yonder, *copies, step=0):
             self.there, self.lon, self.lat, self.here, self.yonder = there, lon, lat, here, yonder
             theirs = rank(lon, lat)
-            self.greets = there & (mine < theirs)
-            self.answers = there & (mine > theirs)
-            self.far = theirs - mine > 25 * 1024
+            ahead = mine < theirs
+            if step == 1:
+                ahead = ahead | (j == seam)
+            if step == -1:
+                ahead = ahead & (j != seam + 1)
+            self.greets = there & ahead
+            self.answers = there & ~ahead
+            self.far = (theirs - mine > 250 * 1024) | (step == 2)
             self.copies = [copy(*c, lon, lat) for c in copies]
 
         def signal(self, sem):
@@ -183,37 +183,31 @@
                 c.start()
 
     below, above, fold = j > 0, j < top, j == top
+    seam = lat_count // 2 if lat_count > 3 else lat_count
+    beside = j != seam
+    e_cols, w_cols = pl.ds(5, 3), pl.ds(8, 3)
     routes = [
+        Route(below, t, j - 1, 2, 3, (state.at[:, 0:3, :], north.at[:, 0:3, :], HN, 2), step=-1),
         Route(
-            below, t, j - 1, 2, 3,
-            (own.at[:, 8:11, :], north.at[:, 0:3, :], HN, 2),
-            (edges.at[:, first], north_edges, BN, 3),
+            above, t, j + 1, 3, 2, (state.at[:, 61:64, :], south.at[:, 5:8, :], HS, 6), step=1
         ),
-        Route(below, east, j - 1, 4, 7, (edges.at[0:8, first], corner_nw, NW, 4)),
-        Route(below, west, j - 1, 5, 6, (edges.at[8:16, first], corner_ne, NE, 5)),
-        Route(
-            above, t, j + 1, 3, 2,
-            (own.at[:, 69:72, :], south.at[:, 5:8, :], HS, 6),
-            (edges.at[:, last], south_edges, BS, 7),
-        ),
-        Route(above, east, j + 1, 6, 5, (edges.at[0:8, last], corner_sw, SW, 8)),
-        Route(above, west, j + 1, 7, 4, (edges.at[8:16, last], corner_se, SE, 9)),
-        Route(
-            fold, mirror, j, 3, 3,
-            (fold_rows.at[:, 0:3, :], north.at[:, 0:3, :], HN, 6),
-            (fold_edges, north_edges, BN, 7),
-        ),
+        Route(below, east, j - 1, 4, 7, (edges.at[e_cols, first], corner_nw.at[5:8, :], NW, 4), step=-1),
+        Route(below, west, j - 1, 5, 6, (edges.at[w_cols, first], corner_ne.at[0:3, :], NE, 5), step=-1),
+        Route(above, east, j + 1, 6, 5, (edges.at[e_cols, last], corner_sw.at[5:8, :], SW, 8), step=1),
+        Route(above, west, j + 1, 7, 4, (edges.at[w_cols, last], corner_se.at[0:3, :], SE, 9), step=1),
+        Route(fold, mirror, j, 3, 3, (fold_rows.at[:, 0:3, :], north.at[:, 0:3, :], HN, 6)),
         Route(
             fold & (mirror_down != t), mirror_down, j, 6, 6,
-            (fold_edges.at[8:16, :], corner_ne, NE, 9),
+            (fold_edges.at[8:11, :], corner_ne.at[0:3, :], NE, 9),
         ),
         Route(
             fold & (mirror_up != t), mirror_up, j, 7, 7,
-            (fold_edges.at[0:8, :], corner_nw, NW, 8),
+            (fold_edges.at[5:8, :], corner_nw.at[5:8, :], NW, 8),
         ),
-        Route(j >= 0, east, j, 0, 1, (edges.at[5:8, :], west_cols.at[5:8, :], HW, 0)),
-        Route(j >= 0, west, j, 1, 0, (edges.at[8:11, :], east_cols.at[0:3, :], HE, 1)),
+        Route(beside, east, j, 0, 1, (edges.at[e_cols, :], west_cols.at[5:8, :], HW, 0)),
+        Route(beside, west, j, 1, 0, (edges.at[w_cols, :], east_cols.at[0:3, :], HE, 1)),
     ]
+    rows_routes, edge_routes = routes[0:2], routes[2:]
 
     barrier = pltpu.get_barrier_semaphore()
     greeted = jnp.int32(0)
@@ -233,6 +227,9 @@
         @pl.when(route.answers)
         def _():
             route.signal(answers.at[route.yonder])
+
+    for route in rows_routes:
+        pl.when(route.answers)(route.send)
 
     own[:, 0:8, :] = jnp.zeros((16, 8, 128), F32)
     own[:, 72:80, :] = jnp.zeros((16, 8, 128), F32)
@@ -242,11 +239,15 @@
         ref[1152:1280, :] = zeros
 
     loads[0].wait()
-
-    for g in range(8):
+    loads[1].wait()
+
+    def turn(g):
         turned = own[:, 8 * g + 8 : 8 * g + 16, :].reshape(128, 128).T
         edges[0:8, 128 * g : 128 * g + 128] = turned[120:128]
         edges[8:16, 128 * g : 128 * g + 128] = turned[0:8]
+
+    turn(0)
+    turn(7)
 
     @pl.when(fold)
     def _():
@@ -265,18 +266,25 @@
             x = jnp.take_along_axis(x, up, axis=0)
             fold_edges[8 - at : 16 - at, :] = jnp.where(lane < 64, -x, x)
 
-    for route in routes:
+    for route in edge_routes[:-2]:
         pl.when(route.answers)(route.send)
 
+    loads[2].wait()
+    for g in range(1, 7):
+        turn(g)
+
+    for route in edge_routes[-2:]:
+        pl.when(route.answers)(route.send)
+
     @pl.when(fold & (mirror_up == t))
     def _():
-        corner_nw[...] = fold_edges[0:8, :]
+        corner_nw[5:8, :] = fold_edges[5:8, :]
 
     @pl.when(fold & (mirror_down == t))
     def _():
-        corner_ne[...] = fold_edges[8:16, :]
-
-    for load in loads[1:]:
+        corner_ne[0:3, :] = fold_edges[8:11, :]
+
+    for load in loads[3:]:
         load.wait()
     bands(taps_one, spread, band_one)
     bands(taps_two, spread, band_two)
@@ -295,6 +303,11 @@
         @pl.when(route.greets & ~route.far)
         def _():
             pl.semaphore_wait(answers.at[route.here], 1)
+            route.send()
+
+    @pl.when(j == seam)
+    def _():
+        for route in routes[-2:]:
             route.send()
 
     for g in range(8):
@@ -361,31 +374,40 @@
     @pl.when(below)
     def _():
         arrive(south.at[:, 5:8, :], HS)
-        arrive(south_edges, BS)
-        arrive(corner_sw, SW)
-        arrive(corner_se, SE)
+        arrive(corner_sw.at[5:8, :], SW)
+        arrive(corner_se.at[0:3, :], SE)
 
     arrive(north.at[:, 0:3, :], HN)
-    arrive(north_edges, BN)
 
     @pl.when(above | (mirror_up != t))
     def _():
-        arrive(corner_nw, NW)
+        arrive(corner_nw.at[5:8, :], NW)
 
     @pl.when(above | (mirror_down != t))
     def _():
-        arrive(corner_ne, NE)
-
+        arrive(corner_ne.at[0:3, :], NE)
+
+    place = iota((8, 128), 0)
+    rows_south = jnp.where(((place >= 5) & below)[None], south[...], 0.0)
+    rows_north = jnp.where((place < 3)[None], north[...], 0.0)
+    south_turned = rows_south.reshape(128, 128).T
+    north_turned = rows_north.reshape(128, 128).T
     strip = jnp.concatenate(
         [
-            jnp.concatenate([south[...], own[:, 64:72, :]], axis=2).reshape(128, 256),
-            jnp.concatenate([own[:, 8:16, :], north[...]], axis=2).reshape(128, 256),
+            jnp.concatenate([rows_south, own[:, 64:72, :]], axis=2).reshape(128, 256),
+            jnp.concatenate([own[:, 8:16, :], rows_north], axis=2).reshape(128, 256),
         ],
         axis=0,
     ).astype(BF16)
     cols = [
         jnp.concatenate(
-            [corner_sw[...], south_edges[8:16, :], south_edges[0:8, :], corner_se[...]], axis=0
+            [
+                jnp.where(below, corner_sw[...], 0.0),
+                south_turned[0:8],
+                south_turned[120:128],
+                jnp.where(below, corner_se[...], 0.0),
+            ],
+            axis=0,
         )
     ]
     for g in range(8):
@@ -397,7 +419,7 @@
         )
     cols.append(
         jnp.concatenate(
-            [corner_nw[...], north_edges[8:16, :], north_edges[0:8, :], corner_ne[...]], axis=0
+            [corner_nw[...], north_turned[0:8], north_turned[120:128], corner_ne[...]], axis=0
         )
     )
     cols = [x.astype(BF16) for x in cols]
@@ -432,8 +454,6 @@
     forcing_north = (across(y, 64)[0] + bias).reshape(8, 8, 128)
     forcing_sides = sides(cols, band_three, range(1, 9)) + bias_rows[2][None]
 
-    place = iota((8, 128), 0)
-    lane = iota((8, 128), 1)
     patches = []
     for g in range(8):
         at = pl.ds(128 * g, 128)
@@ -458,10 +478,10 @@
             x = own[:, 8 * g + 8 : 8 * g + 16, :]
             v = jnp.concatenate([x[4:8]] * 4, axis=0)
             if g == 0:
-                near = jnp.where(place[None] == 0, (0.2 + 0.5 * v) * roll(south[...], 1, 1), 0.0)
+                near = jnp.where(place[None] == 0, (0.2 + 0.5 * v) * roll(rows_south, 1, 1), 0.0)
                 forcing = jnp.where((inner & (place < 3))[None], forcing_south, 0.0)
             else:
-                near = jnp.where(place[None] == 7, (0.2 - 0.5 * v) * roll(north[...], -1, 1), 0.0)
+                near = jnp.where(place[None] == 7, (0.2 - 0.5 * v) * roll(rows_north, -1, 1), 0.0)
                 forcing = jnp.where((inner & (place >= 5))[None], forcing_north, 0.0)
             patch = patch + near
             patch = jnp.concatenate([patch[0:8] + forcing, patch[8:16]], axis=0)
@@ -471,7 +491,9 @@
 
     for route in routes:
 
-        @pl.when(route.there)
+        there = route.there | (j == seam) if route in routes[-2:] else route.there
+
+        @pl.when(there)
         def _():
             for c in route.copies:
                 c.wait_send()
@@ -501,8 +523,6 @@
                 pltpu.VMEM((16, 1024), F32),
                 pltpu.VMEM((8, 1024), F32),
                 pltpu.VMEM((8, 1024), F32),
-                pltpu.VMEM((16, 128), F32),
-                pltpu.VMEM((16, 128), F32),
                 pltpu.VMEM((8, 128), F32),
                 pltpu.VMEM((8, 128), F32),
                 pltpu.VMEM((8, 128), F32),
@@ -516,7 +536,7 @@
                 pltpu.VMEM((3, 128, 128), F32),
                 pltpu.VMEM((1280, 128), BF16),
                 pltpu.VMEM((1280, 128), BF16),
-                pltpu.SemaphoreType.DMA((8,)),
+                pltpu.SemaphoreType.DMA((10,)),
                 pltpu.SemaphoreType.DMA((10,)),
                 pltpu.SemaphoreType.DMA((10,)),
                 pltpu.SemaphoreType.REGULAR((8,)),

time: 23.6 us -> 23.3 us (0.987)
  Pallas kernels: 22.7 us -> 22.4 us
    pallas_call x1, Pallas kernels: 22.7 us -> 22.4 us  [step(): pl.pallas_call(functools.partial(kernel, lon_count, lat_count), out_shape...]
where the time goes in v3:
time: 23.3 us; the launch traced here: 23.2 us
  Pallas kernels  22.4 us (96%)
  local copies, waits for them, and re-layouts  0.8 us (3%)
    pallas_call x1, Pallas kernels, step(): pl.pallas_call(functools.partial(kernel, lon_count, lat_count), out_shape...  22.4 us
    unnamed x1, local copies, waits for them, and re-layouts  0.8 us

profile of v3, /device:TPU:6, one launch (start us, length us, event | category | flops | bytes accessed | tf_op | source)
XLA Modules:
  0.0 23.2 jit_solution(11912957749620345094)
XLA Ops:
  0.0 22.4 %shard_map.82 = f32[16,64,128]{2,1,0:T(8,128)S(1)} custom-call(f32[16,64,128]{2,1,0:T(8,128)} %state.1, s32[64,128]{1,0:T(8,128)} %land_mask.1, bf16[3,3,16,16]{3,2,1,0:T(8,128)(2,1)} %kernel_one.1, f32[16]{0:T(128)} %bias_one.1, bf16[3,3,16,16]{3,2,1,0:T(8,128)(2,1)} %kernel_two.1, f32[16]{0:T(128)} %bias_two.1, bf16[3,3,8,16]{3,2,1,0:T(8,128)(2,1)} %kernel_three.1, ...), custom_call_target="tpu_custom_call" | custom-call | tf_op jit(solution)/shard_map/pallas_call | solution.py:507
  22.4 0.8 %copy.10 = f32[16,64,128]{2,1,0:T(8,128)} copy(f32[16,64,128]{2,1,0:T(8,128)S(1)} %shard_map.82) | data formatting | bytes 1048576

commit v4 on v3

--- a/solution.py
+++ b/solution.py
@@ -160,17 +160,36 @@
         )
 
     class Route:
-        def __init__(self, there, lon, lat, here, yonder, *copies, step=0):
+        def __init__(self, there, lon, lat, here, yonder, *copies, step=0, quiet=False):
             self.there, self.lon, self.lat, self.here, self.yonder = there, lon, lat, here, yonder
             theirs = rank(lon, lat)
             ahead = mine < theirs
+            level = jnp.abs(theirs - mine) < 300 * 1024
+            if here == yonder:
+                both = level
+            else:
+                inside = (lon > 0) & (t > 0) & (lon < lon_count - 1) & (t < lon_count - 1)
+                crossing = (j == seam) if step == -1 else (j == seam - 1) if step == 1 else False
+                both = level & inside & crossing
             if step == 1:
                 ahead = ahead | (j == seam)
             if step == -1:
                 ahead = ahead & (j != seam + 1)
-            self.greets = there & ahead
-            self.answers = there & ~ahead
-            self.far = (theirs - mine > 250 * 1024) | (step == 2)
+            if (here, yonder) == (5, 6):
+                ahead = ahead | ((t == lon_count - 1) & (j == seam))
+            if (here, yonder) == (6, 5):
+                ahead = ahead & ~((t == lon_count - 2) & (j == seam - 1))
+            loud = there & ~jnp.bool_(quiet)
+            self.greets = loud & (both | ahead)
+            self.counts = loud & (both | ~ahead)
+            self.answers = loud & ~both & ~ahead
+            self.awaits = loud & ~both & ahead
+            wraps = (lon - t > 1) | (t - lon > 1)
+            self.far = (theirs - mine > 250 * 1024) | (wraps & (here != yonder))
+            if (here, yonder) == (5, 6):
+                self.awaits = self.awaits & ~((t == lon_count - 1) & (j == seam))
+            if (here, yonder) == (6, 5):
+                self.answers = self.answers & ~((t == lon_count - 2) & (j == seam - 1))
             self.copies = [copy(*c, lon, lat) for c in copies]
 
         def signal(self, sem):
@@ -183,18 +202,37 @@
                 c.start()
 
     below, above, fold = j > 0, j < top, j == top
-    seam = lat_count // 2 if lat_count > 3 else lat_count
-    beside = j != seam
+    seam = lat_count // 2 if lat_count > 3 and lon_count > 3 else 2 * lat_count
+    end = lon_count - 1
+    corner = seam < lat_count
+    at_first = (t == 0) & (j == 0) & corner
+    at_end, at_start = (t == end) & corner, (t == 0) & corner
     e_cols, w_cols = pl.ds(5, 3), pl.ds(8, 3)
-    routes = [
-        Route(below, t, j - 1, 2, 3, (state.at[:, 0:3, :], north.at[:, 0:3, :], HN, 2), step=-1),
-        Route(
-            above, t, j + 1, 3, 2, (state.at[:, 61:64, :], south.at[:, 5:8, :], HS, 6), step=1
-        ),
-        Route(below, east, j - 1, 4, 7, (edges.at[e_cols, first], corner_nw.at[5:8, :], NW, 4), step=-1),
-        Route(below, west, j - 1, 5, 6, (edges.at[w_cols, first], corner_ne.at[0:3, :], NE, 5), step=-1),
-        Route(above, east, j + 1, 6, 5, (edges.at[e_cols, last], corner_sw.at[5:8, :], SW, 8), step=1),
-        Route(above, west, j + 1, 7, 4, (edges.at[w_cols, last], corner_se.at[0:3, :], SE, 9), step=1),
+    route_s = Route(
+        below, t, j - 1, 2, 3, (state.at[:, 0:3, :], north.at[:, 0:3, :], HN, 2),
+        step=-1, quiet=at_end & (j == seam),
+    )
+    route_n = Route(
+        above, t, j + 1, 3, 2, (state.at[:, 61:64, :], south.at[:, 5:8, :], HS, 6),
+        step=1, quiet=at_end & (j == seam - 1),
+    )
+    route_se = Route(
+        below, east, j - 1, 4, 7, (edges.at[e_cols, first], corner_nw.at[5:8, :], NW, 4),
+        step=-1, quiet=at_end & (j == 1),
+    )
+    route_sw = Route(
+        below, west, j - 1, 5, 6, (edges.at[w_cols, first], corner_ne.at[0:3, :], NE, 5),
+        step=-1, quiet=at_start & ((j == seam) | (j == seam + 1)),
+    )
+    route_ne = Route(
+        above, east, j + 1, 6, 5, (edges.at[e_cols, last], corner_sw.at[5:8, :], SW, 8),
+        step=1, quiet=at_end & ((j == seam - 1) | (j == seam)),
+    )
+    route_nw = Route(
+        above, west, j + 1, 7, 4, (edges.at[w_cols, last], corner_se.at[0:3, :], SE, 9),
+        step=1, quiet=at_first,
+    )
+    fold_routes = [
         Route(fold, mirror, j, 3, 3, (fold_rows.at[:, 0:3, :], north.at[:, 0:3, :], HN, 6)),
         Route(
             fold & (mirror_down != t), mirror_down, j, 6, 6,
@@ -204,20 +242,38 @@
             fold & (mirror_up != t), mirror_up, j, 7, 7,
             (fold_edges.at[5:8, :], corner_nw.at[5:8, :], NW, 8),
         ),
-        Route(beside, east, j, 0, 1, (edges.at[e_cols, :], west_cols.at[5:8, :], HW, 0)),
-        Route(beside, west, j, 1, 0, (edges.at[w_cols, :], east_cols.at[0:3, :], HE, 1)),
     ]
-    rows_routes, edge_routes = routes[0:2], routes[2:]
+    route_e = Route(
+        j >= 0, east, j, 0, 1, (edges.at[e_cols, :], west_cols.at[5:8, :], HW, 0),
+        quiet=(j == seam) | (at_end & (j == 0)),
+    )
+    route_w = Route(
+        j >= 0, west, j, 1, 0, (edges.at[w_cols, :], east_cols.at[0:3, :], HE, 1),
+        quiet=(j == seam) | at_first,
+    )
+    rows_routes = [route_s, route_n]
+    corner_routes = [route_se, route_sw, route_ne, route_nw] + fold_routes
+    side_routes = [route_e, route_w]
+    routes = rows_routes + corner_routes + side_routes
 
     barrier = pltpu.get_barrier_semaphore()
     greeted = jnp.int32(0)
     for route in routes:
-        greeted = greeted + route.answers.astype(jnp.int32)
+        greeted = greeted + route.counts.astype(jnp.int32)
 
         @pl.when(route.greets)
         def _():
             route.signal(barrier)
 
+    for host, guest in (((end - 1, 0), (0, 0)), ((end - 1, seam - 1), (0, seam))):
+        greeted = greeted + ((t == host[0]) & (j == host[1]) & corner).astype(jnp.int32)
+
+        @pl.when((t == guest[0]) & (j == guest[1]) & corner)
+        def _():
+            pl.semaphore_signal(
+                barrier, inc=1, device_id={"lon": host[0], "lat": host[1]}, device_id_type=MESH
+            )
+
     @pl.when(greeted > 0)
     def _():
         pl.semaphore_wait(barrier, greeted)
@@ -229,7 +285,7 @@
             route.signal(answers.at[route.yonder])
 
     for route in rows_routes:
-        pl.when(route.answers)(route.send)
+        pl.when(route.counts)(route.send)
 
     own[:, 0:8, :] = jnp.zeros((16, 8, 128), F32)
     own[:, 72:80, :] = jnp.zeros((16, 8, 128), F32)
@@ -266,15 +322,15 @@
             x = jnp.take_along_axis(x, up, axis=0)
             fold_edges[8 - at : 16 - at, :] = jnp.where(lane < 64, -x, x)
 
-    for route in edge_routes[:-2]:
-        pl.when(route.answers)(route.send)
+    for route in corner_routes:
+        pl.when(route.counts)(route.send)
 
     loads[2].wait()
     for g in range(1, 7):
         turn(g)
 
-    for route in edge_routes[-2:]:
-        pl.when(route.answers)(route.send)
+    for route in side_routes:
+        pl.when(route.counts)(route.send)
 
     @pl.when(fold & (mirror_up == t))
     def _():
@@ -300,15 +356,22 @@
 
     for route in routes:
 
-        @pl.when(route.greets & ~route.far)
+        @pl.when(route.awaits & ~route.far)
         def _():
             pl.semaphore_wait(answers.at[route.here], 1)
             route.send()
 
     @pl.when(j == seam)
     def _():
-        for route in routes[-2:]:
-            route.send()
+        route_e.send()
+
+        @pl.when(t > 0)
+        def _():
+            route_w.send()
+
+        @pl.when(t == end)
+        def _():
+            route_ne.send()
 
     for g in range(8):
         x = own[:, 8 * g + 8 : 8 * g + 16, :].reshape(128, 128)
@@ -358,26 +421,84 @@
             ocean = 0.1 * mask[at : at + 8, :].astype(F32)
             out[:, at : at + 8, :] = x + ocean[None] * tendency
 
-    for route in routes:
-
-        @pl.when(route.greets & route.far)
+    for route in [route_e, route_w, route_sw, route_se, route_nw, route_ne] + fold_routes + rows_routes:
+
+        @pl.when(route.awaits & route.far)
         def _():
             pl.semaphore_wait(answers.at[route.here], 1)
             route.send()
 
+        if route is route_w:
+
+            @pl.when(at_start & (j == seam + 1))
+            def _():
+                route_sw.send()
+
     def arrive(dst, slot):
         copy(dst, dst, slot, 0, east, j).wait_recv()
 
-    arrive(west_cols.at[5:8, :], HW)
+    def arrive_west():
+        arrive(west_cols.at[5:8, :], HW)
+
+    def arrive_south():
+        arrive(south.at[:, 5:8, :], HS)
+
+    def arrive_north():
+        arrive(north.at[:, 0:3, :], HN)
+
+    def arrive_sw():
+        arrive(corner_sw.at[5:8, :], SW)
+
+    via_west = at_end & ((j == 0) | (j == seam - 1) | (j == seam))
+    via_sw = at_end & (j == 1)
+    via_south = at_start & (j == seam)
+    via_north = at_first
+
+    @pl.when(via_west)
+    def _():
+        arrive_west()
+
+        @pl.when(j == 0)
+        def _():
+            route_e.send()
+
+        @pl.when(j == seam - 1)
+        def _():
+            route_n.send()
+            route_ne.send()
+
+        @pl.when(j == seam)
+        def _():
+            route_s.send()
+            route_sw.send()
+
+    @pl.when(via_sw)
+    def _():
+        arrive_sw()
+        route_se.send()
+
+    @pl.when(via_south)
+    def _():
+        arrive_south()
+        route_w.send()
+        route_sw.send()
+
+    @pl.when(via_north)
+    def _():
+        arrive_north()
+        route_w.send()
+        route_nw.send()
+
+    pl.when(~via_west)(arrive_west)
     arrive(east_cols.at[0:3, :], HE)
 
     @pl.when(below)
     def _():
-        arrive(south.at[:, 5:8, :], HS)
-        arrive(corner_sw.at[5:8, :], SW)
+        pl.when(~via_south)(arrive_south)
+        pl.when(~via_sw)(arrive_sw)
         arrive(corner_se.at[0:3, :], SE)
 
-    arrive(north.at[:, 0:3, :], HN)
+    pl.when(~via_north)(arrive_north)
 
     @pl.when(above | (mirror_up != t))
     def _():
@@ -491,9 +612,7 @@
 
     for route in routes:
 
-        there = route.there | (j == seam) if route in routes[-2:] else route.there
-
-        @pl.when(there)
+        @pl.when(route.there)
         def _():
             for c in route.copies:
                 c.wait_send()

time: 23.3 us -> 21.4 us (0.918)
  the two profiles are of different devices: /device:TPU:6 before, /device:TPU:31 now
where the time goes in v4:
time: 21.4 us; the launch traced here: 21.2 us
  Pallas kernels  20.4 us (95%)
  local copies, waits for them, and re-layouts  0.8 us (4%)
    pallas_call x1, Pallas kernels, step(): pl.pallas_call(functools.partial(kernel, lon_count, lat_count), out_shape...  20.4 us
    unnamed x1, local copies, waits for them, and re-layouts  0.8 us

profile of v4, /device:TPU:31, one launch (start us, length us, event | category | flops | bytes accessed | tf_op | source)
XLA Modules:
  0.0 21.2 jit_solution(14874366033516454952)
XLA Ops:
  0.0 20.4 %shard_map.82 = f32[16,64,128]{2,1,0:T(8,128)S(1)} custom-call(f32[16,64,128]{2,1,0:T(8,128)} %state.1, s32[64,128]{1,0:T(8,128)} %land_mask.1, bf16[3,3,16,16]{3,2,1,0:T(8,128)(2,1)} %kernel_one.1, f32[16]{0:T(128)} %bias_one.1, bf16[3,3,16,16]{3,2,1,0:T(8,128)(2,1)} %kernel_two.1, f32[16]{0:T(128)} %bias_two.1, bf16[3,3,8,16]{3,2,1,0:T(8,128)(2,1)} %kernel_three.1, ...), custom_call_target="tpu_custom_call" | custom-call | tf_op jit(solution)/shard_map/pallas_call | solution.py:626
  20.4 0.8 %copy.10 = f32[16,64,128]{2,1,0:T(8,128)} copy(f32[16,64,128]{2,1,0:T(8,128)S(1)} %shard_map.82) | data formatting | bytes 1048576

commit v5 on v4

--- a/solution.py
+++ b/solution.py
@@ -25,11 +25,39 @@
     return pltpu.roll(x, shift % x.shape[axis], axis)
 
 
-def bands(taps, spread, band):
+def spread_taps(taps, spread):
     outs = taps.shape[2]
     spreading = (iota((16, 128), 0) == iota((16, 128), 1) // 8).astype(BF16)
     flat = taps[...].reshape(9 * outs, 16)
     spread[0 : 9 * outs, :] = jnp.dot(flat, spreading, preferred_element_type=F32)
+
+
+def tap_rows(spread, outs, c, o):
+    at = [(a * 3 + c) * outs + o for a in range(3)]
+    return [jnp.broadcast_to(spread[i : i + 1, :], (8, 128)) for i in at]
+
+
+def shifted_bands(spread, band, shift):
+    ahead = iota((8, 128), 1) % 8 - iota((8, 128), 0)
+    for c in range(3):
+        for pair in range(8):
+            parts = []
+            for o in (2 * pair, 2 * pair + 1):
+                tap = tap_rows(spread, 16, c, o)
+                groups = []
+                for g in range(2):
+                    part = jnp.zeros((8, 128), F32)
+                    for a in range(3):
+                        part = jnp.where(ahead == shift + a - 1 - 8 * g, tap[a], part)
+                    groups.append(part)
+                parts.append(jnp.concatenate(groups, axis=1))
+            at = c * 128 + pair * 16
+            band[at : at + 16, :] = jnp.concatenate(parts, axis=0).astype(BF16)
+
+
+def bands(taps, spread, band):
+    outs = taps.shape[2]
+    spread_taps(taps, spread)
     ahead = iota((8, 128), 1) % 8 - iota((8, 128), 0)
     for c in range(3):
         for pair in range(8):
@@ -38,10 +66,7 @@
                 if o >= outs:
                     parts.append(jnp.zeros((8, 384), F32))
                     continue
-                tap = []
-                for a in range(3):
-                    at = (a * 3 + c) * outs + o
-                    tap.append(jnp.broadcast_to(spread[at : at + 1, :], (8, 128)))
+                tap = tap_rows(spread, outs, c, o)
                 before = jnp.where(ahead == 7, tap[0], 0.0)
                 centre = jnp.where(
                     ahead == -1,
@@ -104,6 +129,9 @@
     band_one,
     band_two,
     band_three,
+    band_south,
+    band_north,
+    edge_groups,
     bias_full,
     hidden_a,
     hidden_b,
@@ -301,6 +329,8 @@
         turned = own[:, 8 * g + 8 : 8 * g + 16, :].reshape(128, 128).T
         edges[0:8, 128 * g : 128 * g + 128] = turned[120:128]
         edges[8:16, 128 * g : 128 * g + 128] = turned[0:8]
+        if g in (0, 7):
+            edge_groups[g // 7] = turned
 
     turn(0)
     turn(7)
@@ -343,6 +373,8 @@
     for load in loads[3:]:
         load.wait()
     bands(taps_one, spread, band_one)
+    shifted_bands(spread, band_south, 6)
+    shifted_bands(spread, band_north, 2)
     bands(taps_two, spread, band_two)
     bands(taps_three, spread, band_three)
     lane_out = iota((1, 128), 1) // 8
@@ -489,126 +521,137 @@
         route_w.send()
         route_nw.send()
 
-    pl.when(~via_west)(arrive_west)
-    arrive(east_cols.at[0:3, :], HE)
-
-    @pl.when(below)
-    def _():
-        pl.when(~via_south)(arrive_south)
-        pl.when(~via_sw)(arrive_sw)
-        arrive(corner_se.at[0:3, :], SE)
-
-    pl.when(~via_north)(arrive_north)
-
-    @pl.when(above | (mirror_up != t))
-    def _():
-        arrive(corner_nw.at[5:8, :], NW)
-
-    @pl.when(above | (mirror_down != t))
-    def _():
-        arrive(corner_ne.at[0:3, :], NE)
+    def sideways():
+        pl.when(~via_west)(arrive_west)
+        arrive(east_cols.at[0:3, :], HE)
+
+    def southern():
+        @pl.when(below)
+        def _():
+            pl.when(~via_south)(arrive_south)
+            pl.when(~via_sw)(arrive_sw)
+            arrive(corner_se.at[0:3, :], SE)
+
+    def northern():
+        pl.when(~via_north)(arrive_north)
+
+        @pl.when(above | (mirror_up != t))
+        def _():
+            arrive(corner_nw.at[5:8, :], NW)
+
+        @pl.when(above | (mirror_down != t))
+        def _():
+            arrive(corner_ne.at[0:3, :], NE)
 
     place = iota((8, 128), 0)
-    rows_south = jnp.where(((place >= 5) & below)[None], south[...], 0.0)
-    rows_north = jnp.where((place < 3)[None], north[...], 0.0)
-    south_turned = rows_south.reshape(128, 128).T
-    north_turned = rows_north.reshape(128, 128).T
-    strip = jnp.concatenate(
-        [
-            jnp.concatenate([rows_south, own[:, 64:72, :]], axis=2).reshape(128, 256),
-            jnp.concatenate([own[:, 8:16, :], rows_north], axis=2).reshape(128, 256),
-        ],
-        axis=0,
-    ).astype(BF16)
-    cols = [
-        jnp.concatenate(
-            [
-                jnp.where(below, corner_sw[...], 0.0),
-                south_turned[0:8],
-                south_turned[120:128],
-                jnp.where(below, corner_se[...], 0.0),
-            ],
-            axis=0,
-        )
-    ]
-    for g in range(8):
-        at = pl.ds(128 * g, 128)
-        cols.append(
-            jnp.concatenate(
-                [west_cols[:, at], edges[8:16, at], edges[0:8, at], east_cols[:, at]], axis=0
+    lane = iota((8, 128), 1)
+    inner = (lane >= 3) & (lane < 125)
+
+    def taps_on(x, band):
+        return lax.dot_general(x, band, (((1,), (1,)), ((), ())), preferred_element_type=F32)
+
+    def columns():
+        none = jnp.zeros((32, 128), BF16)
+
+        def layer(h, band, i):
+            h = [none] + h + [none]
+            lhs = jnp.concatenate(
+                [jnp.concatenate(h[g : g + 3], axis=1) for g in range(8)], axis=0
             )
-        )
-    cols.append(
-        jnp.concatenate(
-            [corner_nw[...], north_turned[0:8], north_turned[120:128], corner_ne[...]], axis=0
-        )
-    )
-    cols = [x.astype(BF16) for x in cols]
-
-    def sides(cols, band, groups):
-        none = jnp.zeros((32, 128), BF16)
-        padded = [none] + cols + [none]
-        lhs = jnp.concatenate(
-            [jnp.concatenate(padded[g : g + 3], axis=1) for g in groups], axis=0
-        )
-        y = lax.dot_general(
-            lhs, band[...], (((1,), (1,)), ((), ())), preferred_element_type=F32
-        )
-        return down(y, len(groups))
-
-    for band, i in ((band_one, 0), (band_two, 1)):
-        halves = []
-        for at in (128, 0):
-            y = jnp.dot(band[:, at : at + 256], strip, preferred_element_type=F32)
-            bias = bias_full[i]
-            halves.append(
-                jnp.concatenate([silu(v + bias).astype(BF16) for v in across(y, 128)], axis=1)
-            )
-        strip = jnp.concatenate(halves, axis=0)
-        y = silu(sides(cols, band, range(10)) + bias_rows[i][None]).astype(BF16)
-        cols = [y[g] for g in range(10)]
-
-    bias = bias_full[2, 0:64, :]
-    y = jnp.dot(band_last[:, 0:256], strip[:, 0:128], preferred_element_type=F32)
-    forcing_south = (across(y, 64)[0] + bias).reshape(8, 8, 128)
-    y = jnp.dot(band_last[:, 128:384], strip[:, 128:256], preferred_element_type=F32)
-    forcing_north = (across(y, 64)[0] + bias).reshape(8, 8, 128)
-    forcing_sides = sides(cols, band_three, range(1, 9)) + bias_rows[2][None]
-
-    patches = []
-    for g in range(8):
-        at = pl.ds(128 * g, 128)
+            return down(taps_on(lhs, band[...]), 8) + bias_rows[i][None]
+
+        h = []
+        for g in range(8):
+            at = pl.ds(128 * g, 128)
+            parts = [west_cols[:, at], edges[8:16, at], edges[0:8, at], east_cols[:, at]]
+            h.append(jnp.concatenate(parts, axis=0).astype(BF16))
+        for band, i in ((band_one, 0), (band_two, 1)):
+            y = silu(layer(h, band, i)).astype(BF16)
+            h = [y[g] for g in range(8)]
+        f = layer(h, band_three, 2)
 
         def speed(x):
             x = jnp.where(lane < 32, x, 0.0)
             x = x + roll(x, 32, 1)
             return x + roll(x, 64, 1)
 
-        e = edges[0:8, at]
-        w = edges[8:16, at]
-        east_term = jnp.where(place == 7, (0.2 - 0.5 * speed(e)) * roll(east_cols[:, at], -1, 0), 0.0)
-        west_term = jnp.where(place == 0, (0.2 + 0.5 * speed(w)) * roll(west_cols[:, at], 1, 0), 0.0)
-        patches.append(forcing_sides[g, 16:24] + east_term)
-        patches.append(forcing_sides[g, 8:16] + west_term)
-    turned = jnp.concatenate(patches, axis=0).T
-    inner = (lane >= 3) & (lane < 125)
-    for g in range(8):
-        patch = roll(turned, 120 - 16 * g, 1).reshape(16, 8, 128)
-        patch = jnp.where(inner[None], 0.0, patch)
-        if g in (0, 7):
-            x = own[:, 8 * g + 8 : 8 * g + 16, :]
-            v = jnp.concatenate([x[4:8]] * 4, axis=0)
-            if g == 0:
-                near = jnp.where(place[None] == 0, (0.2 + 0.5 * v) * roll(rows_south, 1, 1), 0.0)
-                forcing = jnp.where((inner & (place < 3))[None], forcing_south, 0.0)
-            else:
-                near = jnp.where(place[None] == 7, (0.2 - 0.5 * v) * roll(rows_north, -1, 1), 0.0)
-                forcing = jnp.where((inner & (place >= 5))[None], forcing_north, 0.0)
-            patch = patch + near
-            patch = jnp.concatenate([patch[0:8] + forcing, patch[8:16]], axis=0)
+        parts = []
+        for g in range(8):
+            at = pl.ds(128 * g, 128)
+            fe, fw = f[g, 16:24], f[g, 8:16]
+            if g in (0, 7):
+                kept = lane % 8 >= 3 if g == 0 else lane % 8 < 5
+                fe, fw = jnp.where(kept, fe, 0.0), jnp.where(kept, fw, 0.0)
+            e, w = speed(edges[0:8, at]), speed(edges[8:16, at])
+            e = jnp.where(place == 7, (0.2 - 0.5 * e) * roll(east_cols[:, at], -1, 0), 0.0)
+            w = jnp.where(place == 0, (0.2 + 0.5 * w) * roll(west_cols[:, at], 1, 0), 0.0)
+            parts += [fe + e, fw + w]
+        turned = jnp.concatenate(parts, axis=0).T
+        for g in range(8):
+            patch = roll(turned, 120 - 16 * g, 1).reshape(16, 8, 128)
+            add(g, jnp.where(inner[None], 0.0, patch))
+
+    def add(g, patch):
         at = 8 * g
         ocean = 0.1 * mask[at : at + 8, :].astype(F32)
         out[:, at : at + 8, :] = out[:, at : at + 8, :] + ocean[None] * patch
+
+    def edge(side):
+        if side == "south":
+            g, at, shift, band = 0, pl.ds(0, 128), -2, band_south
+            rows = jnp.where(((place >= 5) & below)[None], south[...], 0.0)
+            ends = [jnp.where(below, x[...], 0.0) for x in (corner_sw, corner_se)]
+            outer, next_to, step, sign = place < 3, place == 0, 1, 0.5
+        else:
+            g, at, shift, band = 7, pl.ds(896, 128), 2, band_north
+            rows = jnp.where((place < 3)[None], north[...], 0.0)
+            ends = [corner_nw[...], corner_ne[...]]
+            outer, next_to, step, sign = place >= 5, place == 7, -1, -0.5
+        beyond = jnp.concatenate([ends[0], rows.reshape(128, 128).T, ends[1]], axis=0)
+        here = jnp.concatenate([west_cols[:, at], edge_groups[g // 7], east_cols[:, at]], axis=0)
+        pair = [beyond, here] if side == "south" else [here, beyond]
+        h = jnp.concatenate(pair, axis=1).astype(BF16)
+        for taps, i in (
+            (band[...], 0),
+            (band_two[:, 128:256], 1),
+            (band_three[:, 128:256], 2),
+        ):
+            y = taps_on(h, taps)
+            y = roll(y[:, 0:128], 1, 0) + y[:, 128:256] + roll(y[:, 256:384], -1, 0) + bias_rows[i]
+            h = silu(y).astype(BF16)
+        forcing = roll(y[8:136].T[0:64].reshape(8, 8, 128), shift, 1)
+        forcing = jnp.where(outer[None], forcing, 0.0)
+        x = own[:, 8 * g + 8 : 8 * g + 16, :]
+        v = jnp.concatenate([x[4:8]] * 4, axis=0)
+        near = jnp.where(next_to[None], (0.2 + sign * v) * roll(rows, step, 1), 0.0)
+        add(g, jnp.concatenate([near[0:8] + forcing, near[8:16]], axis=0))
+
+    @pl.when(t == 0)
+    def _():
+        sideways()
+        southern()
+        northern()
+        columns()
+        edge("south")
+        edge("north")
+
+    @pl.when((t > 0) & (j == seam))
+    def _():
+        sideways()
+        northern()
+        columns()
+        edge("north")
+        southern()
+        edge("south")
+
+    @pl.when((t > 0) & (j != seam))
+    def _():
+        sideways()
+        southern()
+        columns()
+        edge("south")
+        northern()
+        edge("north")
 
     for route in routes:
 
@@ -652,6 +695,9 @@
                 pltpu.VMEM((384, 384), BF16),
                 pltpu.VMEM((384, 384), BF16),
                 pltpu.VMEM((384, 384), BF16),
+                pltpu.VMEM((384, 256), BF16),
+                pltpu.VMEM((384, 256), BF16),
+                pltpu.VMEM((2, 128, 128), F32),
                 pltpu.VMEM((3, 128, 128), F32),
                 pltpu.VMEM((1280, 128), BF16),
                 pltpu.VMEM((1280, 128), BF16),

time: 21.4 us -> 20.9 us (0.977)
  the two profiles are of different devices: /device:TPU:31 before, /device:TPU:6 now
where the time goes in v5:
time: 20.9 us; the launch traced here: 20.8 us
  Pallas kernels  20 us (96%)
  local copies, waits for them, and re-layouts  0.8 us (4%)
    pallas_call x1, Pallas kernels, step(): pl.pallas_call(functools.partial(kernel, lon_count, lat_count), out_shape...  20 us
    unnamed x1, local copies, waits for them, and re-layouts  0.8 us

profile of v5, /device:TPU:6, one launch (start us, length us, event | category | flops | bytes accessed | tf_op | source)
XLA Modules:
  0.0 20.8 jit_solution(12355790888027634051)
XLA Ops:
  0.0 20.0 %shard_map.82 = f32[16,64,128]{2,1,0:T(8,128)S(1)} custom-call(f32[16,64,128]{2,1,0:T(8,128)} %state.1, s32[64,128]{1,0:T(8,128)} %land_mask.1, bf16[3,3,16,16]{3,2,1,0:T(8,128)(2,1)} %kernel_one.1, f32[16]{0:T(128)} %bias_one.1, bf16[3,3,16,16]{3,2,1,0:T(8,128)(2,1)} %kernel_two.1, f32[16]{0:T(128)} %bias_two.1, bf16[3,3,8,16]{3,2,1,0:T(8,128)(2,1)} %kernel_three.1, ...), custom_call_target="tpu_custom_call" | custom-call | tf_op jit(solution)/shard_map/pallas_call | solution.py:669
  20.0 0.8 %copy.10 = f32[16,64,128]{2,1,0:T(8,128)} copy(f32[16,64,128]{2,1,0:T(8,128)S(1)} %shard_map.82) | data formatting | bytes 1048576

commit v6 on v5

--- a/solution.py
+++ b/solution.py
@@ -168,7 +168,7 @@
         load.start()
 
     def rank(lon, lat):
-        z, y, x, core = (lat // 4) * 6 + lon // 16, (lon % 16) // 2, lat % 4, lon % 2
+        z, y, x, core = (lat >> 2) * 6 + (lon >> 4), (lon & 15) >> 1, lat & 3, lon & 1
         guess = jnp.where(z < 6, 128 + 150 * z, 940 + 30 * z) + 45 * x - 41 * core
         guess = guess + jnp.where(y < 4, 57 * y, 430 - 35 * y)
         guess = jnp.where(lon + lat == 0, 1050, guess)
@@ -214,6 +214,8 @@
             self.awaits = loud & ~both & ahead
             wraps = (lon - t > 1) | (t - lon > 1)
             self.far = (theirs - mine > 250 * 1024) | (wraps & (here != yonder))
+            if (here, yonder) == (1, 0):
+                self.far = self.far | ((t == lon_count - 1) & (j == seam - 1))
             if (here, yonder) == (5, 6):
                 self.awaits = self.awaits & ~((t == lon_count - 1) & (j == seam))
             if (here, yonder) == (6, 5):
@@ -250,11 +252,11 @@
     )
     route_sw = Route(
         below, west, j - 1, 5, 6, (edges.at[w_cols, first], corner_ne.at[0:3, :], NE, 5),
-        step=-1, quiet=at_start & ((j == seam) | (j == seam + 1)),
+        step=-1, quiet=at_start & (j == seam + 1),
     )
     route_ne = Route(
         above, east, j + 1, 6, 5, (edges.at[e_cols, last], corner_sw.at[5:8, :], SW, 8),
-        step=1, quiet=at_end & ((j == seam - 1) | (j == seam)),
+        step=1, quiet=at_end & (j == seam),
     )
     route_nw = Route(
         above, west, j + 1, 7, 4, (edges.at[w_cols, last], corner_se.at[0:3, :], SE, 9),
@@ -293,7 +295,7 @@
         def _():
             route.signal(barrier)
 
-    for host, guest in (((end - 1, 0), (0, 0)), ((end - 1, seam - 1), (0, seam))):
+    for host, guest in (((end - 1, 0), (0, 0)),):
         greeted = greeted + ((t == host[0]) & (j == host[1]) & corner).astype(jnp.int32)
 
         @pl.when((t == guest[0]) & (j == guest[1]) & corner)
@@ -323,7 +325,6 @@
         ref[1152:1280, :] = zeros
 
     loads[0].wait()
-    loads[1].wait()
 
     def turn(g):
         turned = own[:, 8 * g + 8 : 8 * g + 16, :].reshape(128, 128).T
@@ -333,6 +334,10 @@
             edge_groups[g // 7] = turned
 
     turn(0)
+    for route in corner_routes[0:2]:
+        pl.when(route.counts)(route.send)
+
+    loads[1].wait()
     turn(7)
 
     @pl.when(fold)
@@ -352,7 +357,7 @@
             x = jnp.take_along_axis(x, up, axis=0)
             fold_edges[8 - at : 16 - at, :] = jnp.where(lane < 64, -x, x)
 
-    for route in corner_routes:
+    for route in corner_routes[2:]:
         pl.when(route.counts)(route.send)
 
     loads[2].wait()
@@ -453,19 +458,6 @@
             ocean = 0.1 * mask[at : at + 8, :].astype(F32)
             out[:, at : at + 8, :] = x + ocean[None] * tendency
 
-    for route in [route_e, route_w, route_sw, route_se, route_nw, route_ne] + fold_routes + rows_routes:
-
-        @pl.when(route.awaits & route.far)
-        def _():
-            pl.semaphore_wait(answers.at[route.here], 1)
-            route.send()
-
-        if route is route_w:
-
-            @pl.when(at_start & (j == seam + 1))
-            def _():
-                route_sw.send()
-
     def arrive(dst, slot):
         copy(dst, dst, slot, 0, east, j).wait_recv()
 
@@ -497,7 +489,6 @@
         @pl.when(j == seam - 1)
         def _():
             route_n.send()
-            route_ne.send()
 
         @pl.when(j == seam)
         def _():
@@ -509,11 +500,23 @@
         arrive_sw()
         route_se.send()
 
+    for route in [route_e, route_w, route_sw, route_se, route_nw, route_ne] + fold_routes + rows_routes:
+
+        @pl.when(route.awaits & route.far)
+        def _():
+            pl.semaphore_wait(answers.at[route.here], 1)
+            route.send()
+
+        if route is route_w:
+
+            @pl.when(at_start & (j == seam + 1))
+            def _():
+                route_sw.send()
+
     @pl.when(via_south)
     def _():
         arrive_south()
         route_w.send()
-        route_sw.send()
 
     @pl.when(via_north)
     def _():
@@ -521,6 +524,10 @@
         route_w.send()
         route_nw.send()
 
+    place = iota((8, 128), 0)
+    lane = iota((8, 128), 1)
+    inner = (lane >= 3) & (lane < 125)
+
     def sideways():
         pl.when(~via_west)(arrive_west)
         arrive(east_cols.at[0:3, :], HE)
@@ -543,9 +550,6 @@
         def _():
             arrive(corner_ne.at[0:3, :], NE)
 
-    place = iota((8, 128), 0)
-    lane = iota((8, 128), 1)
-    inner = (lane >= 3) & (lane < 125)
 
     def taps_on(x, band):
         return lax.dot_general(x, band, (((1,), (1,)), ((), ())), preferred_element_type=F32)
@@ -568,7 +572,9 @@
         for band, i in ((band_one, 0), (band_two, 1)):
             y = silu(layer(h, band, i)).astype(BF16)
             h = [y[g] for g in range(8)]
+            yield
         f = layer(h, band_three, 2)
+        yield
 
         def speed(x):
             x = jnp.where(lane < 32, x, 0.0)
@@ -619,6 +625,7 @@
             y = taps_on(h, taps)
             y = roll(y[:, 0:128], 1, 0) + y[:, 128:256] + roll(y[:, 256:384], -1, 0) + bias_rows[i]
             h = silu(y).astype(BF16)
+            yield
         forcing = roll(y[8:136].T[0:64].reshape(8, 8, 128), shift, 1)
         forcing = jnp.where(outer[None], forcing, 0.0)
         x = own[:, 8 * g + 8 : 8 * g + 16, :]
@@ -626,32 +633,33 @@
         near = jnp.where(next_to[None], (0.2 + sign * v) * roll(rows, step, 1), 0.0)
         add(g, jnp.concatenate([near[0:8] + forcing, near[8:16]], axis=0))
 
+    def together(*pieces):
+        pieces = list(pieces)
+        while pieces:
+            pieces = [p for p in pieces if next(p, pieces) is not pieces]
+
     @pl.when(t == 0)
     def _():
         sideways()
         southern()
         northern()
-        columns()
-        edge("south")
-        edge("north")
+        together(edge("south"), edge("north"), columns())
 
     @pl.when((t > 0) & (j == seam))
     def _():
         sideways()
         northern()
-        columns()
-        edge("north")
+        together(edge("north"), columns())
         southern()
-        edge("south")
+        together(edge("south"))
 
     @pl.when((t > 0) & (j != seam))
     def _():
         sideways()
         southern()
-        columns()
-        edge("south")
+        together(edge("south"), columns())
         northern()
-        edge("north")
+        together(edge("north"))
 
     for route in routes:
 

time: 20.9 us -> 20.5 us (0.981)
  Pallas kernels: 20 us -> 19.4 us
    pallas_call x1, Pallas kernels: 20 us -> 19.4 us  [step(): pl.pallas_call(functools.partial(kernel, lon_count, lat_count), out_shape...]
where the time goes in v6:
time: 20.5 us; the launch traced here: 20.2 us
  Pallas kernels  19.4 us (95%)
  local copies, waits for them, and re-layouts  0.8 us (4%)
    pallas_call x1, Pallas kernels, step(): pl.pallas_call(functools.partial(kernel, lon_count, lat_count), out_shape...  19.4 us
    unnamed x1, local copies, waits for them, and re-layouts  0.8 us

profile of v6, /device:TPU:6, one launch (start us, length us, event | category | flops | bytes accessed | tf_op | source)
XLA Modules:
  0.0 20.2 jit_solution(12258968781853454785)
XLA Ops:
  0.0 19.4 %shard_map.82 = f32[16,64,128]{2,1,0:T(8,128)S(1)} custom-call(f32[16,64,128]{2,1,0:T(8,128)} %state.1, s32[64,128]{1,0:T(8,128)} %land_mask.1, bf16[3,3,16,16]{3,2,1,0:T(8,128)(2,1)} %kernel_one.1, f32[16]{0:T(128)} %bias_one.1, bf16[3,3,16,16]{3,2,1,0:T(8,128)(2,1)} %kernel_two.1, f32[16]{0:T(128)} %bias_two.1, bf16[3,3,8,16]{3,2,1,0:T(8,128)(2,1)} %kernel_three.1, ...), custom_call_target="tpu_custom_call" | custom-call | tf_op jit(solution)/shard_map/pallas_call | solution.py:677
  19.4 0.8 %copy.10 = f32[16,64,128]{2,1,0:T(8,128)} copy(f32[16,64,128]{2,1,0:T(8,128)S(1)} %shard_map.82) | data formatting | bytes 1048576

commit v7 on v6

--- a/solution.py
+++ b/solution.py
@@ -90,7 +90,7 @@
 
 
 def down(y, groups):
-    z = [y[:, 128 * c : 128 * c + 128].reshape(groups, 32, 128) for c in range(3)]
+    z = [y[:, 128 * c : 128 * c + 128].reshape(groups, -1, 128) for c in range(3)]
     return roll(z[0], 1, 1) + z[1] + roll(z[2], -1, 1)
 
 
@@ -475,7 +475,6 @@
 
     via_west = at_end & ((j == 0) | (j == seam - 1) | (j == seam))
     via_sw = at_end & (j == 1)
-    via_south = at_start & (j == seam)
     via_north = at_first
 
     @pl.when(via_west)
@@ -513,10 +512,11 @@
             def _():
                 route_sw.send()
 
-    @pl.when(via_south)
-    def _():
-        arrive_south()
-        route_w.send()
+        if route is route_nw:
+
+            @pl.when(at_start & (j == seam))
+            def _():
+                route_w.send()
 
     @pl.when(via_north)
     def _():
@@ -528,33 +528,35 @@
     lane = iota((8, 128), 1)
     inner = (lane >= 3) & (lane < 125)
 
-    def sideways():
+    def from_se():
+        pl.when(below)(lambda: arrive(corner_se.at[0:3, :], SE))
+
+    def from_south():
+        pl.when(below)(arrive_south)
+
+    def from_sw():
+        pl.when(below & ~via_sw)(arrive_sw)
+
+    def from_ne():
+        pl.when(above | (mirror_down != t))(lambda: arrive(corner_ne.at[0:3, :], NE))
+
+    def from_north():
+        pl.when(~via_north)(arrive_north)
+
+    def from_nw():
+        pl.when(above | (mirror_up != t))(lambda: arrive(corner_nw.at[5:8, :], NW))
+
+    def from_west():
         pl.when(~via_west)(arrive_west)
+
+    def from_east():
         arrive(east_cols.at[0:3, :], HE)
-
-    def southern():
-        @pl.when(below)
-        def _():
-            pl.when(~via_south)(arrive_south)
-            pl.when(~via_sw)(arrive_sw)
-            arrive(corner_se.at[0:3, :], SE)
-
-    def northern():
-        pl.when(~via_north)(arrive_north)
-
-        @pl.when(above | (mirror_up != t))
-        def _():
-            arrive(corner_nw.at[5:8, :], NW)
-
-        @pl.when(above | (mirror_down != t))
-        def _():
-            arrive(corner_ne.at[0:3, :], NE)
 
 
     def taps_on(x, band):
         return lax.dot_general(x, band, (((1,), (1,)), ((), ())), preferred_element_type=F32)
 
-    def columns():
+    def columns(kept_lanes, west=True):
         none = jnp.zeros((32, 128), BF16)
 
         def layer(h, band, i):
@@ -567,7 +569,8 @@
         h = []
         for g in range(8):
             at = pl.ds(128 * g, 128)
-            parts = [west_cols[:, at], edges[8:16, at], edges[0:8, at], east_cols[:, at]]
+            beside = west_cols[:, at] if west else jnp.zeros((8, 128), F32)
+            parts = [beside, edges[8:16, at], edges[0:8, at], east_cols[:, at]]
             h.append(jnp.concatenate(parts, axis=0).astype(BF16))
         for band, i in ((band_one, 0), (band_two, 1)):
             y = silu(layer(h, band, i)).astype(BF16)
@@ -575,11 +578,6 @@
             yield
         f = layer(h, band_three, 2)
         yield
-
-        def speed(x):
-            x = jnp.where(lane < 32, x, 0.0)
-            x = x + roll(x, 32, 1)
-            return x + roll(x, 64, 1)
 
         parts = []
         for g in range(8):
@@ -590,33 +588,85 @@
                 fe, fw = jnp.where(kept, fe, 0.0), jnp.where(kept, fw, 0.0)
             e, w = speed(edges[0:8, at]), speed(edges[8:16, at])
             e = jnp.where(place == 7, (0.2 - 0.5 * e) * roll(east_cols[:, at], -1, 0), 0.0)
-            w = jnp.where(place == 0, (0.2 + 0.5 * w) * roll(west_cols[:, at], 1, 0), 0.0)
-            parts += [fe + e, fw + w]
+            if west:
+                w = jnp.where(place == 0, (0.2 + 0.5 * w) * roll(west_cols[:, at], 1, 0), 0.0)
+                fw = fw + w
+            parts += [fe + e, fw]
         turned = jnp.concatenate(parts, axis=0).T
         for g in range(8):
             patch = roll(turned, 120 - 16 * g, 1).reshape(16, 8, 128)
-            add(g, jnp.where(inner[None], 0.0, patch))
+            add(g, jnp.where(kept_lanes[None], patch, 0.0))
+
+    def speed(x):
+        x = jnp.where(lane < 32, x, 0.0)
+        x = x + roll(x, 32, 1)
+        return x + roll(x, 64, 1)
+
+    def western():
+        none = jnp.zeros((16, 128), BF16)
+        south_rows, north_rows = rows_at("south"), rows_at("north")
+        h = [jnp.concatenate([jnp.where(below, corner_sw[...], 0.0), south_rows.reshape(128, 128).T[0:8]], axis=0)]
+        for g in range(8):
+            at = pl.ds(128 * g, 128)
+            h.append(jnp.concatenate([west_cols[:, at], edges[8:16, at]], axis=0))
+        h.append(jnp.concatenate([corner_nw[...], north_rows.reshape(128, 128).T[0:8]], axis=0))
+        h = [x.astype(BF16) for x in h]
+        for band, i, groups in ((band_one, 0, range(10)), (band_two, 1, range(10)), (band_three, 2, range(1, 9))):
+            h = [none] + h + [none]
+            lhs = [jnp.concatenate(h[g : g + 3], axis=1) for g in groups]
+            y = down(taps_on(jnp.concatenate(lhs, axis=0), band[...]), len(lhs)) + bias_rows[i][None]
+            z = silu(y).astype(BF16)
+            h = [z[g] for g in range(len(lhs))]
+        parts = []
+        for g in range(8):
+            at = pl.ds(128 * g, 128)
+            w = (0.2 + 0.5 * speed(edges[8:16, at])) * roll(west_cols[:, at], 1, 0)
+            parts.append(y[g, 8:16] + jnp.where(place == 0, w, 0.0))
+        turned = jnp.concatenate(parts + [jnp.zeros((64, 128), F32)], axis=0).T
+        for g in range(8):
+            patch = roll(turned, -8 * g, 1).reshape(16, 8, 128)
+            add(g, jnp.where((lane < 3)[None], patch, 0.0))
+
+    def rows_at(side):
+        if side == "south":
+            return jnp.where(((place >= 5) & below)[None], south[...], 0.0)
+        return jnp.where((place < 3)[None], north[...], 0.0)
 
     def add(g, patch):
         at = 8 * g
         ocean = 0.1 * mask[at : at + 8, :].astype(F32)
         out[:, at : at + 8, :] = out[:, at : at + 8, :] + ocean[None] * patch
 
-    def edge(side):
+    def edge(side, kept_lanes, west=True, corner=True):
         if side == "south":
             g, at, shift, band = 0, pl.ds(0, 128), -2, band_south
-            rows = jnp.where(((place >= 5) & below)[None], south[...], 0.0)
-            ends = [jnp.where(below, x[...], 0.0) for x in (corner_sw, corner_se)]
+            rows = rows_at(side)
+            ends = [corner_sw, corner_se]
             outer, next_to, step, sign = place < 3, place == 0, 1, 0.5
         else:
             g, at, shift, band = 7, pl.ds(896, 128), 2, band_north
-            rows = jnp.where((place < 3)[None], north[...], 0.0)
-            ends = [corner_nw[...], corner_ne[...]]
+            rows = rows_at(side)
+            ends = [corner_nw, corner_ne]
             outer, next_to, step, sign = place >= 5, place == 7, -1, -0.5
+        blank = jnp.zeros((8, 128), F32)
+        ends = [x[...] if come else blank for x, come in zip(ends, (west, corner))]
+        if side == "south":
+            ends = [jnp.where(below, x, 0.0) for x in ends]
         beyond = jnp.concatenate([ends[0], rows.reshape(128, 128).T, ends[1]], axis=0)
-        here = jnp.concatenate([west_cols[:, at], edge_groups[g // 7], east_cols[:, at]], axis=0)
+        beside = west_cols[:, at] if west else blank
+        here = jnp.concatenate([beside, edge_groups[g // 7], east_cols[:, at]], axis=0)
         pair = [beyond, here] if side == "south" else [here, beyond]
         h = jnp.concatenate(pair, axis=1).astype(BF16)
+        for y in edge_layers(h, band):
+            yield
+        forcing = roll(y[8:136].T[0:64].reshape(8, 8, 128), shift, 1)
+        forcing = jnp.where((outer & kept_lanes)[None], forcing, 0.0)
+        x = own[:, 8 * g + 8 : 8 * g + 16, :]
+        v = jnp.concatenate([x[4:8]] * 4, axis=0)
+        near = jnp.where(next_to[None], (0.2 + sign * v) * roll(rows, step, 1), 0.0)
+        add(g, jnp.concatenate([near[0:8] + forcing, near[8:16]], axis=0))
+
+    def edge_layers(h, band):
         for taps, i in (
             (band[...], 0),
             (band_two[:, 128:256], 1),
@@ -625,41 +675,60 @@
             y = taps_on(h, taps)
             y = roll(y[:, 0:128], 1, 0) + y[:, 128:256] + roll(y[:, 256:384], -1, 0) + bias_rows[i]
             h = silu(y).astype(BF16)
-            yield
-        forcing = roll(y[8:136].T[0:64].reshape(8, 8, 128), shift, 1)
-        forcing = jnp.where(outer[None], forcing, 0.0)
-        x = own[:, 8 * g + 8 : 8 * g + 16, :]
-        v = jnp.concatenate([x[4:8]] * 4, axis=0)
-        near = jnp.where(next_to[None], (0.2 + sign * v) * roll(rows, step, 1), 0.0)
-        add(g, jnp.concatenate([near[0:8] + forcing, near[8:16]], axis=0))
+            yield y
+
+    def north_east():
+        beyond = rows_at("north").reshape(128, 128).T[104:128]
+        beyond = jnp.concatenate([beyond, corner_ne[...]], axis=0)
+        here = jnp.concatenate([edge_groups[1, 104:128, :], east_cols[:, 896:1024]], axis=0)
+        for y in edge_layers(jnp.concatenate([here, beyond], axis=1).astype(BF16), band_north):
+            pass
+        turned = jnp.concatenate([jnp.zeros((104, 128), F32), y[0:24]], axis=0).T
+        forcing = roll(turned[0:64].reshape(8, 8, 128), 2, 1)
+        forcing = jnp.where(((place >= 5) & (lane >= 125))[None], forcing, 0.0)
+        ocean = 0.1 * mask[56:64, :].astype(F32)
+        out[0:8, 56:64, :] = out[0:8, 56:64, :] + ocean[None] * forcing
 
     def together(*pieces):
         pieces = list(pieces)
         while pieces:
             pieces = [p for p in pieces if next(p, pieces) is not pieces]
 
+    everywhere = lane >= 0
+    outside = (lane < 3) | (lane >= 125)
+
     @pl.when(t == 0)
     def _():
-        sideways()
-        southern()
-        northern()
-        together(edge("south"), edge("north"), columns())
+        for wait in (from_east, from_south, from_se, from_north, from_ne):
+            wait()
+        together(
+            edge("south", lane >= 3, west=False),
+            edge("north", lane >= 3, west=False),
+            columns(lane >= 125, west=False),
+        )
+        for wait in (from_west, from_sw, from_nw):
+            wait()
+        western()
 
     @pl.when((t > 0) & (j == seam))
     def _():
-        sideways()
-        northern()
-        together(edge("north"), columns())
-        southern()
-        together(edge("south"))
+        for wait in (from_west, from_east, from_north, from_nw, from_ne):
+            wait()
+        together(edge("north", everywhere), columns(outside))
+        for wait in (from_south, from_sw, from_se):
+            wait()
+        together(edge("south", everywhere))
 
     @pl.when((t > 0) & (j != seam))
     def _():
-        sideways()
-        southern()
-        together(edge("south"), columns())
-        northern()
-        together(edge("north"))
+        for wait in (from_west, from_east, from_south, from_sw, from_se):
+            wait()
+        together(edge("south", everywhere), columns(outside))
+        from_north()
+        from_nw()
+        together(edge("north", lane < 125, corner=False))
+        from_ne()
+        north_east()
 
     for route in routes:
 

time: 20.5 us -> 20.4 us (level)
  the two profiles are of different devices: /device:TPU:6 before, /device:TPU:31 now
where the time goes in v7:
time: 20.4 us; the launch traced here: 20.3 us
  Pallas kernels  19.5 us (96%)
  local copies, waits for them, and re-layouts  0.8 us (4%)
    pallas_call x1, Pallas kernels, step(): pl.pallas_call(functools.partial(kernel, lon_count, lat_count), out_shape...  19.5 us
    unnamed x1, local copies, waits for them, and re-layouts  0.8 us

profile of v7, /device:TPU:31, one launch (start us, length us, event | category | flops | bytes accessed | tf_op | source)
XLA Modules:
  0.0 20.3 jit_solution(11754660672905110975)
XLA Ops:
  0.0 19.5 %shard_map.82 = f32[16,64,128]{2,1,0:T(8,128)S(1)} custom-call(f32[16,64,128]{2,1,0:T(8,128)} %state.1, s32[64,128]{1,0:T(8,128)} %land_mask.1, bf16[3,3,16,16]{3,2,1,0:T(8,128)(2,1)} %kernel_one.1, f32[16]{0:T(128)} %bias_one.1, bf16[3,3,16,16]{3,2,1,0:T(8,128)(2,1)} %kernel_two.1, f32[16]{0:T(128)} %bias_two.1, bf16[3,3,8,16]{3,2,1,0:T(8,128)(2,1)} %kernel_three.1, ...), custom_call_target="tpu_custom_call" | custom-call | tf_op jit(solution)/shard_map/pallas_call | solution.py:746
  19.5 0.8 %copy.10 = f32[16,64,128]{2,1,0:T(8,128)} copy(f32[16,64,128]{2,1,0:T(8,128)S(1)} %shard_map.82) | data formatting | bytes 1048576

commit v8 on v7

--- a/solution.py
+++ b/solution.py
@@ -164,8 +164,14 @@
             ]
         )
     ]
-    for load in loads:
-        load.start()
+    row_seam = lat_count // 2 if lat_count > 3 and lon_count > 3 else 2 * lat_count
+    loads[0].start()
+
+    def load_rest():
+        for load in loads[1:]:
+            load.start()
+
+    pl.when(j != row_seam)(load_rest)
 
     def rank(lon, lat):
         z, y, x, core = (lat >> 2) * 6 + (lon >> 4), (lon & 15) >> 1, lat & 3, lon & 1
@@ -199,6 +205,12 @@
                 inside = (lon > 0) & (t > 0) & (lon < lon_count - 1) & (t < lon_count - 1)
                 crossing = (j == seam) if step == -1 else (j == seam - 1) if step == 1 else False
                 both = level & inside & crossing
+            if (here, yonder) == (6, 5):
+                spared = (j == seam - 1) & ((t & 15) == 7) & (2 * t < lon_count)
+                both, ahead = both & ~spared, ahead | spared
+            if (here, yonder) == (5, 6):
+                spared = (j == seam) & ((t & 15) == 8) & (2 * t < lon_count)
+                both, ahead = both & ~spared, ahead & ~spared
             if step == 1:
                 ahead = ahead | (j == seam)
             if step == -1:
@@ -216,6 +228,10 @@
             self.far = (theirs - mine > 250 * 1024) | (wraps & (here != yonder))
             if (here, yonder) == (1, 0):
                 self.far = self.far | ((t == lon_count - 1) & (j == seam - 1))
+            if (here, yonder) == (6, 5):
+                self.awaits, self.there = self.awaits & ~spared, there & ~spared
+            if (here, yonder) == (5, 6):
+                self.answers = self.answers & ~spared
             if (here, yonder) == (5, 6):
                 self.awaits = self.awaits & ~((t == lon_count - 1) & (j == seam))
             if (here, yonder) == (6, 5):
@@ -281,8 +297,12 @@
         j >= 0, west, j, 1, 0, (edges.at[w_cols, :], east_cols.at[0:3, :], HE, 1),
         quiet=(j == seam) | at_first,
     )
+    stands_in = (j == seam - 1) & ((t & 15) == 8) & (2 * t < lon_count)
+    for_neighbour = copy(
+        west_cols.at[5:8, last], corner_sw.at[5:8, :], SW, 10, t, j + 1
+    )
     rows_routes = [route_s, route_n]
-    corner_routes = [route_se, route_sw, route_ne, route_nw] + fold_routes
+    corner_routes = [route_sw, route_se, route_ne, route_nw] + fold_routes
     side_routes = [route_e, route_w]
     routes = rows_routes + corner_routes + side_routes
 
@@ -316,6 +336,8 @@
 
     for route in rows_routes:
         pl.when(route.counts)(route.send)
+
+    pl.when(j == row_seam)(load_rest)
 
     own[:, 0:8, :] = jnp.zeros((16, 8, 128), F32)
     own[:, 72:80, :] = jnp.zeros((16, 8, 128), F32)
@@ -518,6 +540,11 @@
             def _():
                 route_w.send()
 
+    @pl.when(stands_in)
+    def _():
+        arrive_west()
+        for_neighbour.start()
+
     @pl.when(via_north)
     def _():
         arrive_north()
@@ -547,7 +574,7 @@
         pl.when(above | (mirror_up != t))(lambda: arrive(corner_nw.at[5:8, :], NW))
 
     def from_west():
-        pl.when(~via_west)(arrive_west)
+        pl.when(~via_west & ~stands_in)(arrive_west)
 
     def from_east():
         arrive(east_cols.at[0:3, :], HE)
@@ -736,6 +763,8 @@
         def _():
             for c in route.copies:
                 c.wait_send()
+
+    pl.when(stands_in)(lambda: for_neighbour.wait_send())
 
 
 def solution(mesh):
@@ -779,7 +808,7 @@
                 pltpu.VMEM((1280, 128), BF16),
                 pltpu.VMEM((1280, 128), BF16),
                 pltpu.SemaphoreType.DMA((10,)),
-                pltpu.SemaphoreType.DMA((10,)),
+                pltpu.SemaphoreType.DMA((11,)),
                 pltpu.SemaphoreType.DMA((10,)),
                 pltpu.SemaphoreType.REGULAR((8,)),
             ],

time: 20.4 us -> 20.4 us (level)
  no operation moved by 1% of the time
where the time goes in v8:
time: 20.4 us; the launch traced here: 20.3 us
  Pallas kernels  19.5 us (96%)
  local copies, waits for them, and re-layouts  0.8 us (4%)
    pallas_call x1, Pallas kernels, step(): pl.pallas_call(functools.partial(kernel, lon_count, lat_count), out_shape...  19.5 us
    unnamed x1, local copies, waits for them, and re-layouts  0.8 us

profile of v8, /device:TPU:31, one launch (start us, length us, event | category | flops | bytes accessed | tf_op | source)
XLA Modules:
  0.0 20.3 jit_solution(15916910516803428976)
XLA Ops:
  0.0 19.5 %shard_map.82 = f32[16,64,128]{2,1,0:T(8,128)S(1)} custom-call(f32[16,64,128]{2,1,0:T(8,128)} %state.1, s32[64,128]{1,0:T(8,128)} %land_mask.1, bf16[3,3,16,16]{3,2,1,0:T(8,128)(2,1)} %kernel_one.1, f32[16]{0:T(128)} %bias_one.1, bf16[3,3,16,16]{3,2,1,0:T(8,128)(2,1)} %kernel_two.1, f32[16]{0:T(128)} %bias_two.1, bf16[3,3,8,16]{3,2,1,0:T(8,128)(2,1)} %kernel_three.1, ...), custom_call_target="tpu_custom_call" | custom-call | tf_op jit(solution)/shard_map/pallas_call | solution.py:775
  19.5 0.8 %copy.10 = f32[16,64,128]{2,1,0:T(8,128)} copy(f32[16,64,128]{2,1,0:T(8,128)S(1)} %shard_map.82) | data formatting | bytes 1048576
